TPU v7x, 128 devices: a whole 4x4x4 slice. The times are simulated.
128 devices in a mesh: seq: 64 (over y, x, z), head: 2 (over core).
Axes of the slice: x: 4, y: 4, z: 4, core: 2. Of those that a mesh axis runs over, the one named last changes fastest.
Arguments:
- residual: bfloat16 [8192, 2304], P('seq'), may hold values from -40 to 40
- kda_query: bfloat16 [8192, 2048], P('seq', 'head'), may hold values from -6 to 6
- kda_key: bfloat16 [8192, 2048], P('seq', 'head'), may hold values from -6 to 6
- kda_value: bfloat16 [8192, 2048], P('seq', 'head'), may hold values from -6 to 6
- log_decay: float32 [8192, 2048], P('seq', 'head'), may hold values from -1 to 0
- beta_logit: float32 [8192, 16], P('seq', 'head'), may hold values from -8 to 3
- out_gate: bfloat16 [8192, 2048], P('seq', 'head'), may hold values from -8 to 8
- out_gain: float32 [128], replicated, may hold values from 0.25 to 1.75
- out_weight: bfloat16 [2048, 2304], P('head'), may hold values from -0.125 to 0.125
- hidden_gain: float32 [2304], replicated, may hold values from 0.25 to 1.75
- query_weight: bfloat16 [2304, 2048], P(None, 'head'), may hold values from -32 to 32
- latent_weight: bfloat16 [2304, 512], replicated, may hold values from -3 to 3
- latent_gain: float32 [512], replicated, may hold values from 0.25 to 1.75
- key_up_weight: bfloat16 [512, 2048], P(None, 'head'), may hold values from -2 to 2
- value_up_weight: bfloat16 [512, 2048], P(None, 'head'), may hold values from -0.25 to 0.25
Outputs:
- hidden: bfloat16 [8192, 2304], P('seq')
- attended: bfloat16 [8192, 2048], P('seq', 'head')
All inputs are finite; a program needn't handle non-finite values.
Results may differ from a plain program's by a relative error of at most 0.0105.
Values may be sent and summed in bfloat16 or wider, within the bound.
A program may use at most 192 MiB of HBM per device.

v0:
```python
import jax
import jax.numpy as jnp
from jax import lax
from jax.sharding import PartitionSpec as P

HD = 128
BLOCK_LEN = 64


EPS = 1e-06
PRECISION_HIGH = lax.Precision.HIGHEST


def carried_in(value, axis, join, neutral):
    count, mine = (lax.axis_size(axis), lax.axis_index(axis))
    pieces = jax.tree.map(lambda part: lax.all_gather(part, axis), value)
    subtotal = jax.tree.map(
        lambda part, zero: jnp.full_like(part, 0) + jnp.asarray(zero, part.dtype), value, neutral
    )

    def lap(position, subtotal):
        longer = join(subtotal, jax.tree.map(lambda part: part[position], pieces))
        return jax.tree.map(lambda new, old: jnp.where(position < mine, new, old), longer, subtotal)

    return lax.fori_loop(0, count - 1, lap, subtotal)


def rms_scale(values):
    return values * lax.rsqrt(jnp.mean(values * values, axis=-1, keepdims=True) + EPS)


def unit_length(values):
    return values * lax.rsqrt(jnp.sum(values * values, axis=-1, keepdims=True) + EPS)


def compose_pair(earlier, later):
    matrix = jnp.einsum("hij,hjk->hik", later[0], earlier[0], precision=PRECISION_HIGH)
    offset = jnp.einsum("hij,hjk->hik", later[0], earlier[1], precision=PRECISION_HIGH) + later[1]
    return (matrix, offset)


def block_terms(kda_query, kda_key, kda_value, log_decay, beta_logit):
    row_count, heads_here = beta_logit.shape
    head_width = kda_query.shape[1] // heads_here
    blocks = row_count // BLOCK_LEN

    def arrange(values):
        return (
            values.astype(jnp.float32)
            .reshape(blocks, BLOCK_LEN, heads_here, head_width)
            .transpose(0, 2, 1, 3)
        )

    queries = unit_length(arrange(kda_query))
    key_rows = unit_length(arrange(kda_key))
    values = arrange(kda_value)
    summed = jnp.cumsum(arrange(log_decay), axis=2)
    growth = jnp.exp(summed)
    key_fwd = key_rows * growth
    key_back = key_rows * jnp.exp(-summed)
    query_fwd = queries * growth
    write_rate = (
        jax.nn.sigmoid(beta_logit)
        .reshape(blocks, BLOCK_LEN, heads_here)
        .transpose(0, 2, 1)[..., None]
    )
    later_index = jnp.arange(BLOCK_LEN)[:, None]
    earlier_index = jnp.arange(BLOCK_LEN)[None, :]
    strict = earlier_index < later_index
    through = earlier_index <= later_index
    coupling = jnp.einsum("nhtd,nhsd->nhts", key_fwd, key_back, precision=PRECISION_HIGH)
    system = jnp.eye(BLOCK_LEN, dtype=jnp.float32) + write_rate * jnp.where(strict, coupling, 0.0)
    right_side = jnp.concatenate([write_rate * values, write_rate * key_fwd], axis=-1)
    solved = jax.scipy.linalg.solve_triangular(system, right_side, lower=True, unit_diagonal=True)
    written = solved[..., :head_width]
    removal = solved[..., head_width:]
    closing = growth[:, :, -1, :][..., None]
    identity = jnp.eye(head_width, dtype=jnp.float32)
    transition = closing * (
        identity - jnp.einsum("nhsk,nhsj->nhkj", key_back, removal, precision=PRECISION_HIGH)
    )
    offset = closing * jnp.einsum("nhsk,nhsv->nhkv", key_back, written, precision=PRECISION_HIGH)
    local_mix = jnp.where(
        through, jnp.einsum("nhtd,nhsd->nhts", query_fwd, key_back, precision=PRECISION_HIGH), 0.0
    )
    base_out = jnp.einsum("nhts,nhsv->nhtv", local_mix, written, precision=PRECISION_HIGH)
    carried = query_fwd - jnp.einsum(
        "nhts,nhsk->nhtk", local_mix, removal, precision=PRECISION_HIGH
    )
    return (transition, offset, base_out, carried)


def body(
    residual,
    kda_query,
    kda_key,
    kda_value,
    log_decay,
    beta_logit,
    out_gate,
    out_gain,
    out_weight,
    hidden_gain,
    query_weight,
    latent_weight,
    latent_gain,
    key_up_weight,
    value_up_weight,
):
    row_count, heads_here = beta_logit.shape
    head_width = kda_query.shape[1] // heads_here
    transition, offset, base_out, carried = block_terms(
        kda_query, kda_key, kda_value, log_decay, beta_logit
    )
    eye_heads = jnp.broadcast_to(
        jnp.eye(head_width, dtype=jnp.float32), (heads_here, head_width, head_width)
    )
    zero_state = jnp.zeros((heads_here, head_width, head_width), jnp.float32)

    def compose(running, element):
        return (compose_pair(running, element), running)

    shard_pair, before = lax.scan(compose, (eye_heads, zero_state), (transition, offset))
    prefix = carried_in(
        (shard_pair[0], shard_pair[1]), "seq", compose_pair, (eye_heads, zero_state)
    )
    incoming = prefix[1]

    def advance(memory_state, element):
        step_trans, step_offset, output_per_token, carry_per_token = element
        output_per_token = output_per_token + jnp.einsum(
            "ypw,ywb->ypb", carry_per_token, memory_state, precision=PRECISION_HIGH
        )
        memory_state = (
            jnp.einsum("hij,hjk->hik", step_trans, memory_state, precision=PRECISION_HIGH)
            + step_offset
        )
        return (memory_state, output_per_token)

    _, kda_raw = lax.scan(advance, incoming, (transition, offset, base_out, carried))
    kda_raw = kda_raw.transpose(0, 2, 1, 3).reshape(row_count, heads_here, head_width)
    gate_value = jax.nn.sigmoid(
        out_gate.astype(jnp.float32).reshape(row_count, heads_here, head_width)
    )
    gated = (
        (rms_scale(kda_raw) * out_gain * gate_value)
        .reshape(row_count, heads_here * head_width)
        .astype(jnp.bfloat16)
    )
    partial_sum = jnp.dot(gated, out_weight, preferred_element_type=jnp.float32)
    summed_out = residual.astype(jnp.float32) + lax.psum(partial_sum, "head")
    hidden = lax.optimization_barrier(summed_out.astype(jnp.bfloat16))
    normed = (rms_scale(hidden.astype(jnp.float32)) * hidden_gain).astype(jnp.bfloat16)
    queries_mla = jnp.dot(normed, query_weight, preferred_element_type=jnp.float32).astype(
        jnp.bfloat16
    )
    queries_mla = queries_mla.reshape(row_count, -1, HD)
    heads_mla = queries_mla.shape[1]
    first_row = lax.axis_index("seq") * row_count
    query_pos = first_row + jnp.arange(row_count, dtype=jnp.int32)
    last_pos = first_row + row_count - 1
    score_scale = HD ** (-0.5)
    start_state = (
        jnp.full((heads_mla, row_count), -1e30, jnp.float32),
        jnp.zeros((heads_mla, row_count), jnp.float32),
        jnp.zeros((heads_mla, row_count, HD), jnp.float32),
    )
    latent_raw = jnp.dot(normed, latent_weight, preferred_element_type=jnp.float32)
    piece = lax.all_gather(
        (rms_scale(latent_raw) * latent_gain).astype(jnp.bfloat16), "seq", axis=0, tiled=True
    )
    key_pos = jnp.arange(piece.shape[0], dtype=jnp.int32)

    def update(memory_state):
        row_max, row_total, accum_out = memory_state
        count = piece.shape[0]
        keys_up = (
            jnp.dot(piece, key_up_weight, preferred_element_type=jnp.float32)
            .astype(jnp.bfloat16)
            .reshape(count, heads_mla, HD)
        )
        values_up = (
            jnp.dot(piece, value_up_weight, preferred_element_type=jnp.float32)
            .astype(jnp.bfloat16)
            .reshape(count, heads_mla, HD)
        )
        scores = (
            jnp.einsum("qhd,khd->hqk", queries_mla, keys_up, preferred_element_type=jnp.float32)
            * score_scale
        )
        visible = (key_pos[None, :] <= query_pos[:, None])[None]
        scores = jnp.where(visible, scores, -1e30)
        new_max = jnp.maximum(row_max, jnp.max(scores, axis=-1))
        weights = jnp.where(visible, jnp.exp(scores - new_max[..., None]), 0.0)
        row_total = jnp.sum(weights, axis=-1)
        mixed = jnp.einsum(
            "hqk,khd->hqd",
            weights.astype(jnp.bfloat16),
            values_up,
            preferred_element_type=jnp.float32,
        )
        accum_out = mixed
        return (new_max, row_total, accum_out)

    result = lax.cond(
        jnp.min(key_pos) <= last_pos, update, lambda memory_state: memory_state, start_state
    )
    row_max, row_total, accum_out = result
    attended = (
        (accum_out / row_total[..., None])
        .transpose(1, 0, 2)
        .reshape(row_count, heads_mla * HD)
        .astype(jnp.bfloat16)
    )
    return (hidden, attended)


def solution(mesh):
    in_specs = (
        P("seq", None),
        P("seq", "head"),
        P("seq", "head"),
        P("seq", "head"),
        P("seq", "head"),
        P("seq", "head"),
        P("seq", "head"),
        P(),
        P("head", None),
        P(),
        P(None, "head"),
        P(),
        P(),
        P(None, "head"),
        P(None, "head"),
    )
    out_specs = (P("seq", None), P("seq", "head"))
    return jax.shard_map(body, mesh=mesh, in_specs=in_specs, out_specs=out_specs, check_vma=False)
```

profile of v0, /device:TPU:24, one launch (start us, length us, event | category | flops | bytes accessed | tf_op | source)
XLA Modules:
  0.0 916.8 jit_solution(13083463317457860037)
XLA Ops:
  9.9 13.0 %fusion.55 = f32[2,8,64,128]{3,1,2,0:T(8,128)S(1)} fusion(f32[2,64,8,128]{3,2,1,0:T(8,128)S(1)} %bitcast.188), kind=kOutput, calls=%fused_computation.76 | output fusion | flops 8257536 | bytes 1048576 | tf_op jit(solution)/shard_map/jit(cumsum)/reduce_window_sum | solution.py:57
  27.5 3.2 fusion.44
  30.7 80.0 %custom-call.4 = f32[2,8,1,64,64]{3,4,2,1,0:T(8,128)} custom-call(f32[2,8,1,64,64]{4,3,2,1,0:T(8,128)} %fusion.44), custom_call_target="InvertDiagBlocksLowerTriangular" | custom-call | tf_op jit(solution)/shard_map/jit(_solve_triangular)/vmap(vmap())/triangular_solve | solution.py:74
  114.0 3.0 convolution_multiply_fusion
  117.0 3.0 fusion.39
  120.9 12.1 %while.40 = (s32[]{:T(128)}, f32[8,128,128]{2,1,0:T(8,128)}, f32[8,128,128]{2,1,0:T(8,128)}, f32[2,8,128,128]{3,2,1,0:T(8,128)S(1)}, f32[2,8,128,128]{3,2,1,0:T(8,128)}, /*index=5*/s32[]{:T(128)}, s32[]{:T(128)}) while((s32[]{:T(128)}, f32[8,128,128]{2,1,0:T(8,128)}, f32[8,128,128]{2,1,0:T(8,128)}, ...), condition=%wide.region_3.4_spmd.clone, body=%wide.region_2.0_spmd.clone.sunk | while | flops 402915328 | bytes 5768283 | solution.py:123
  140.2 2.8 convolution_subtract_fusion.1
  143.0 153.1 %all-gather.8.cloned.1.call-done = f32[512,128,128]{2,1,0:T(8,128)} async-done(((f32[8,128,128]{2,1,0:T(8,128)}), f32[512,128,128]{2,1,0:T(8,128)}) %all-gather.8.cloned.1.call-update) | async-done | bytes 33554448 | tf_op jit(solution)/shard_map/all_gather | solution.py:16
  296.1 163.3 %all-gather.10.cloned.1.call-done = f32[512,128,128]{2,1,0:T(8,128)} async-done(((f32[8,128,128]{2,1,0:T(8,128)}), f32[512,128,128]{2,1,0:T(8,128)}) %all-gather.10.cloned.1.call-update) | async-done | bytes 33554448 | tf_op jit(solution)/shard_map/all_gather | solution.py:16
  459.4 233.5 %while.41 = (s32[]{:T(128)}, f32[8,128,128]{2,1,0:T(8,128)}, s32[]{:T(128)}, f32[64,8,128,128]{3,2,1,0:T(8,128)}, f32[64,8,128,128]{3,2,1,0:T(8,128)}, /*index=5*/s32[]{:T(128)}, s32[]{:T(128)}) while((s32[]{:T(128)}, f32[8,128,128]{2,1,0:T(8,128)}, s32[]{:T(128)}, f32[64,8,128,128]{3,2,1,0:T(8,128)}, ...), condition=%wide.region_5.6_spmd.clone, body=%wide.region_4.5_spmd.clone.sunk | while | flops 201850880 | bytes 3672671 | solution.py:25
  460.4 2.7 fusion.126
  464.1 2.7 fusion.126
  467.9 2.7 fusion.126
  471.6 2.7 fusion.126
  479.0 2.7 fusion.126
  482.7 2.7 fusion.126
  486.4 2.7 fusion.126
  490.1 2.7 fusion.126
  493.8 2.7 fusion.126
  497.5 2.7 fusion.126
  501.2 2.7 fusion.126
  504.9 2.7 fusion.126
  508.6 2.7 fusion.126
  512.3 2.7 fusion.126
  516.0 2.7 fusion.126
  523.4 2.7 fusion.126
  530.9 2.7 fusion.126
  534.6 2.7 fusion.126
  538.3 2.7 fusion.126
  542.0 2.7 fusion.126
  545.7 2.7 fusion.126
  549.4 2.7 fusion.126
  553.1 2.7 fusion.126
  556.8 2.7 fusion.126
  560.5 2.7 fusion.126
  567.9 2.7 fusion.126
  575.3 2.7 fusion.126
  579.0 2.7 fusion.126
  582.7 2.7 fusion.126
  586.4 2.7 fusion.126
  590.1 2.7 fusion.126
  593.9 2.7 fusion.126
  597.6 2.7 fusion.126
  601.3 2.7 fusion.126
  605.0 2.7 fusion.126
  612.4 2.7 fusion.126
  619.8 2.7 fusion.126
  623.5 2.7 fusion.126
  627.2 2.7 fusion.126
  630.9 2.7 fusion.126
  634.6 2.7 fusion.126
  649.4 2.7 fusion.126
  692.9 11.7 %while.39 = (s32[]{:T(128)}, f32[8,128,128]{2,1,0:T(8,128)}, f32[2,8,64,128]{3,2,1,0:T(8,128)}, f32[2,8,128,128]{3,2,1,0:T(8,128)S(1)}, f32[2,8,128,128]{3,2,1,0...) while((s32[]{:T(128)}, f32[8,128,128]{2,1,0:T(8,128)}, ...), condition=%wide.region_8.9_spmd, body=%wide.region_7.8_spmd.sunk | while | flops 302186496 | bytes 4458581 | solution.py:140
  707.5 4.4 fusion.66
  712.2 24.9 %all-reduce.2.cloned.1.call-done = f32[128,2304]{1,0:T(8,128)} async-done(((f32[128,2304]{1,0:T(8,128)}), f32[128,2304]{1,0:T(8,128)}) %all-reduce.2.cloned.1.call-update) | async-done | bytes 1179664 | tf_op jit(solution)/shard_map/psum | solution.py:151
  740.3 3.2 convolution_convert_fusion.2
  743.5 77.4 %all-gather.6.cloned.1.call-done = bf16[8192,512]{1,0:T(8,128)(2,1)} async-done(((bf16[128,512]{1,0:T(8,128)(2,1)}), bf16[8192,512]{1,0:T(8,128)(2,1)}) %all-gather.6.cloned.1.call-update) | async-done | bytes 8388624 | tf_op jit(solution)/shard_map/all_gather | solution.py:169
  820.9 87.3 %conditional.1 = (f32[8,128]{1,0:T(8,128)S(1)}, f32[8,128,128]{2,1,0:T(8,128)}) conditional(s32[]{:T(128)} %convert_element_type.71, () %tuple.41, (s32[8192]{0:T(1024)S(1)}, s32[]{:T(128)}, s32[128]{0:T(128)S(1)}, bf16[8192,512]{1,0:T(8,128)(2,1)}, bf16[512,1024]{1,0:T(8,128)(2,1)}, /*index=5*/bf16[128,1024]{1,0:T(8,128)(2,1)S(1)}, ...), branch_computations={%region_13.14_spmd, %region_14.17_spmd} | conditional | flops 21601714176 | bytes 195880496 | solution.py:205
  820.9 3.7 broadcast_compare_fusion
  824.6 14.9 %convolution_convert_fusion.1 = bf16[8192,1024]{0,1:T(8,128)(2,1)} fusion(bf16[8192,512]{1,0:T(8,128)(2,1)} %get-tuple-element.175, bf16[512,1024]{1,0:T(8,128)(2,1)} %get-tuple-element.195), kind=kOutput, calls=%fused_computation.18 | convolution fusion | flops 8598323200 | bytes 26214400 | tf_op jit(solution)/shard_map/cond/branch_1_fun/dot_general | solution.py:178
  839.5 18.8 %fusion.8 = (f32[8,128]{1,0:T(8,128)S(1)}, f32[8,8192,128]{2,1,0:T(8,128)}) fusion(pred[128,8192]{0,1:T(8,128)(4,1)S(1)} %broadcast_compare_fusion, bf16[8192,8,128]{0,2,1:T(8,128)(2,1)} %bitcast.177, bf16[128,1024]{1,0:T(8,128)(2,1)S(1)} %get-tuple-element.177), kind=kOutput, calls=%fused_computation.12 | convolution fusion | flops 2172648448 | bytes 51646464 | tf_op jit(solution)/shard_map/cond/branch_1_fun/qhd,khd->hqk/dot_general | solution.py:188
  858.4 14.9 %convolution_convert_fusion = bf16[8192,1024]{0,1:T(8,128)(2,1)} fusion(bf16[8192,512]{1,0:T(8,128)(2,1)} %get-tuple-element.175, bf16[512,1024]{1,0:T(8,128)(2,1)S(1)} %copy-done.10), kind=kOutput, calls=%fused_computation.17 | convolution fusion | flops 8598323200 | bytes 26214400 | tf_op jit(solution)/shard_map/cond/branch_1_fun/dot_general | solution.py:183
  873.2 20.3 %fusion.11 = f32[8,128,128]{2,1,0:T(8,128)} fusion(bf16[8192,8,128]{0,2,1:T(8,128)(2,1)} %bitcast.197, f32[8,8192,128]{2,1,0:T(8,128)} %get-tuple-element.268, f32[8,128]{1,0:T(8,128)S(1)} %broadcast_maximum_fusion, pred[128,8192]{0,1:T(8,128)(4,1)S(1)} %broadcast_compare_fusion), kind=kOutput, calls=%fused_computation.15 | convolution fusion | flops 2189426688 | bytes 51908608 | tf_op jit(solution)/shard_map/cond/branch_1_fun/hqk,khd->hqd/dot_general | solution.py:196
  893.5 14.7 %fusion.10 = f32[8,128]{1,0:T(8,128)S(1)} fusion(f32[8,8192,128]{2,1,0:T(8,128)} %get-tuple-element.268, f32[8,128]{1,0:T(8,128)S(1)} %broadcast_maximum_fusion, pred[128,8192]{0,1:T(8,128)(4,1)S(1)} %broadcast_compare_fusion), kind=kLoop, calls=%fused_computation.14 | loop fusion | flops 41942016 | bytes 34611200 | tf_op jit(solution)/shard_map/cond/branch_1_fun/reduce_sum | solution.py:195
  (173 shorter events, 172.1 us)
Async XLA Ops:
  7.2 731.7 %copy-start = (bf16[2304,512]{1,0:T(8,128)(2,1)S(1)}, bf16[2304,512]{1,0:T(8,128)(2,1)}, u32[]{:S(2)}) copy-start(bf16[2304,512]{1,0:T(8,128)(2,1)} %param.34) | copy-start | bytes 7077892
  7.2 288.9 %all-gather.8.cloned.1.call-start = ((), (), s32[]{:S(2)}) async-start(), calls=%async_computation.2 | async-start | bytes 34078720 | tf_op jit(solution)/shard_map/all_gather | solution.py:16
  8.5 1.4 copy-start.5
  23.0 91.0 %copy-start.2 = (f32[2,8,64,128]{3,1,2,0:T(8,128)}, f32[2,8,64,128]{3,1,2,0:T(8,128)S(1)}, u32[]{:S(2)}) copy-start(f32[2,8,64,128]{3,1,2,0:T(8,128)S(1)} %fusion.55) | copy-start | bytes 1572868
  27.5 86.5 %copy-start.3 = (f32[2,8,64,128]{3,2,1,0:T(8,128)}, f32[2,8,64,128]{3,2,1,0:T(8,128)S(1)}, u32[]{:S(2)}) copy-start(f32[2,8,64,128]{3,2,1,0:T(8,128)S(1)} %get-tuple-element.270) | copy-start | bytes 1572868
  114.0 3.0 copy-start.4
  120.0 15.3 %copy-start.9 = (f32[128]{0:T(128)S(1)}, f32[128]{0:T(128)}, u32[]{:S(2)}) copy-start(f32[128]{0:T(128)} %param.30) | copy-start | bytes 1540
  133.0 326.4 %all-gather.10.cloned.1.call-start = ((), (), s32[]{:S(2)}) async-start(), calls=%async_computation.3 | async-start | bytes 34078720 | tf_op jit(solution)/shard_map/all_gather | solution.py:16
  133.7 603.4 %all-reduce.2.cloned.1.call-start = ((), (), s32[]{:S(2)}) async-start(), calls=%async_computation | async-start | bytes 2359296 | tf_op jit(solution)/shard_map/psum | solution.py:151
  692.9 46.0 %copy-start.7 = (f32[2304]{0:T(1024)S(1)}, f32[2304]{0:T(1024)}, u32[]{:S(2)}) copy-start(f32[2304]{0:T(1024)} %param.32) | copy-start | bytes 27652
  692.9 46.6 %copy-start.8 = (f32[512]{0:T(512)S(1)}, f32[512]{0:T(512)}, u32[]{:S(2)}) copy-start(f32[512]{0:T(512)} %param.35) | copy-start | bytes 6148
  711.9 109.0 %all-gather.6.cloned.1.call-start = ((), (), s32[]{:S(2)}) async-start(), calls=%async_computation.1 | async-start | bytes 8519680 | tf_op jit(solution)/shard_map/all_gather | solution.py:169
  738.7 82.2 %copy-start.6 = (bf16[128,2304]{1,0:T(8,128)(2,1)}, bf16[128,2304]{1,0:T(8,128)(2,1)S(1)}, u32[]{:S(2)}) copy-start(bf16[128,2304]{1,0:T(8,128)(2,1)S(1)} %add_convert_fusion) | copy-start | bytes 1769476
  839.5 18.8 %copy-start.10 = (bf16[512,1024]{1,0:T(8,128)(2,1)S(1)}, bf16[512,1024]{1,0:T(8,128)(2,1)}, u32[]{:S(2)}) copy-start(bf16[512,1024]{1,0:T(8,128)(2,1)} %get-tuple-element.196) | copy-start | bytes 3145732 | tf_op jit(solution)/shard_map/cond
  908.2 2.1 copy-start.1
Sparse Core Ops, SparseCore 0:
  133.1 162.9 all-gather.7
  298.9 160.4 all-gather.9
  712.1 25.0 all-reduce.1
  740.9 79.9 all-gather.5
where the time goes:
time: 924 us; the launch traced here: 917 us
  waiting for transfers between devices  420 us (45%)
  matrix products  281 us (30%)
  other arithmetic  124 us (13%)
  local copies, waits for them, and re-layouts  76.8 us (8%)
  between operations  14.1 us (2%)
    all_gather x2, waiting for transfers between devices, carried_in(): pieces = jax.tree.map(lambda part: lax.all_gather(part, axis), value)  316 us
    dot_general x65, matrix products, compose_pair(): jnp.einsum('hij,hjk->hik', later[0], earlier[1], precision=PRECISION_HIGH)  173 us
    another operation x2, other arithmetic, block_terms(): jax.scipy.linalg.solve_triangular(system, right_side, lower=True, unit_di...  80 us
    all_gather x1, waiting for transfers between devices, body(): lax.all_gather((rms_scale(latent_raw) * latent_gain).astype(jnp.bfloat16)...  77.4 us
    while x69, local copies, waits for them, and re-layouts  71.9 us
    psum x1, waiting for transfers between devices, body(): summed_out = residual.astype(jnp.float32) + lax.psum(partial_sum, 'head')  24.9 us
    dot_general x1, matrix products, update(): jnp.einsum('hqk,khd->hqd', weights.astype(jnp.bfloat16), values_up, prefe...  20.3 us
    dot_general x1, matrix products, update(): jnp.einsum('qhd,khd->hqk', queries_mla, keys_up, preferred_element_type=j...  18.8 us
  transfers between devices with their start and end apart: 4, of which 4 were waited for; matrix products, arithmetic and copies ran while one was open for 1% of the time, Pallas kernels for 0%

commit v1 on v0

v1 whole, which is shorter than its diff:
```python
import jax
import jax.numpy as jnp
from jax import lax
from jax.sharding import PartitionSpec as P
from jax.experimental import pallas as pl
from jax.experimental.pallas import tpu as pltpu

F32 = jnp.float32
BF16 = jnp.bfloat16
W = 128
EPS = 1e-06


def halves(x):
    high = x.astype(BF16)
    return high, (x - high.astype(F32)).astype(BF16)


def mm(a, b):
    return jnp.dot(a, b, preferred_element_type=F32)


def mm_nt(a, b):
    return lax.dot_general(a, b, (((1,), (1,)), ((), ())), preferred_element_type=F32)


def wide(x):
    high, low = halves(x)
    return jnp.concatenate([high, low], axis=1)


def mm4(a, b):
    n = b.shape[1]
    right = wide(b)
    out = mm(wide(a), jnp.concatenate([right, right], axis=0))
    return out[:, :n] + out[:, n:]


def mm4_nt(a, b):
    n = b.shape[0]
    high, low = halves(b)
    right = jnp.concatenate(
        [jnp.concatenate([high, high], axis=1), jnp.concatenate([low, low], axis=1)], axis=0
    )
    out = mm_nt(wide(a), right)
    return out[:, :n] + out[:, n:]


def iota(shape, axis):
    return lax.broadcasted_iota(jnp.int32, shape, axis)


def delta_kernel(q_ref, k_ref, v_ref, ld_ref, beta_ref, msg_ref, base_ref, carry_ref):
    rows = q_ref.shape[0]
    heads = q_ref.shape[1] // W
    ti, si = iota((rows, rows), 0), iota((rows, rows), 1)
    ones = jnp.where(si <= ti, 1.0, 0.0).astype(BF16)
    strict = si < ti
    through = si <= ti
    eye = jnp.where(si == ti, 1.0, 0.0)
    rates = 1.0 / (1.0 + jnp.exp(-beta_ref[...]))

    def stage_one(h):
        cols = slice(h * W, (h + 1) * W)
        ld = ld_ref[:, cols]
        high, rest = halves(ld)
        low = (ld - high.astype(F32) - rest.astype(F32)).astype(BF16)
        cum = mm(ones, high) + (mm(ones, rest) + mm(ones, low))
        mid = cum[rows // 2 - 1 : rows // 2, :]
        end = cum[rows - 1 : rows, :]
        key = k_ref[:, cols].astype(F32)
        key = key * lax.rsqrt(jnp.sum(key * key, axis=-1, keepdims=True) + EPS)
        query = q_ref[:, cols].astype(F32)
        query = query * lax.rsqrt(jnp.sum(query * query, axis=-1, keepdims=True) + EPS)
        forward = jnp.exp(cum - mid)
        mixed = mm4_nt(
            jnp.concatenate([key * forward, query * forward], axis=0), key * jnp.exp(mid - cum)
        )
        rate = rates[:, h : h + 1]
        lower = jnp.where(strict, mixed[:rows], 0.0) * rate
        mix = jnp.where(through, mixed[rows:], 0.0)
        growth = jnp.exp(cum)
        right = jnp.concatenate(
            [rate * v_ref[:, cols].astype(F32), rate * (key * growth)], axis=1
        )
        tail = (key * jnp.exp(end - cum)).T
        return lower, mix, right, tail, query * growth, jnp.exp(end)

    def invert(lowers):
        level = jnp.logical_and((ti // 2) == (si // 2), strict)
        found = [eye - jnp.where(level, low, 0.0) for low in lowers]
        size = 2
        while size < rows:
            level = jnp.logical_and((ti // (2 * size)) == (si // (2 * size)),
                                    (ti // size) > (si // size))
            inner = [mm4(jnp.where(level, low, 0.0), x) for low, x in zip(lowers, found)]
            found = [x - mm4(x, y) for x, y in zip(found, inner)]
            size *= 2
        return found

    group = 4
    for start in range(0, heads, group):
        made = [stage_one(h) for h in range(start, start + group)]
        inverses = invert([m[0] for m in made])
        for h in range(start, start + group):
            _, mix, right, tail, query, closing = made[h - start]
            solved = mm4(inverses[h - start], right)
            state = mm4(tail, solved)
            out = mm4(mix, solved)
            cols = slice(h * W, (h + 1) * W)
            base_ref[:, cols] = out[:, :W]
            carry_ref[:, cols] = (query - out[:, W:]).astype(BF16)
            msg_ref[h, :W, :W] = state[:, W:].astype(BF16)
            msg_ref[h, :W, W:] = state[:, :W].astype(BF16)
            msg_ref[h, W:, :] = pack_diag(closing)


def pack_diag(closing):
    high, rest = halves(closing)
    r = iota((16, W), 0)
    block = jnp.where(r == 0, high.astype(F32), jnp.where(r == 1, rest.astype(F32), 0.0))
    return jnp.concatenate([block, jnp.zeros((16, W), F32)], axis=1).astype(BF16)


def delta_terms(q, k, v, ld, beta):
    rows, heads = beta.shape
    vm = pl.BlockSpec(memory_space=pltpu.VMEM)
    return pl.pallas_call(
        delta_kernel,
        out_shape=(
            jax.ShapeDtypeStruct((heads, W + 16, 2 * W), BF16),
            jax.ShapeDtypeStruct((rows, heads * W), F32),
            jax.ShapeDtypeStruct((rows, heads * W), BF16),
        ),
        in_specs=[vm] * 5,
        out_specs=(vm, vm, vm),
        compiler_params=pltpu.CompilerParams(vmem_limit_bytes=48 * 2**20),
        name="delta_terms",
    )(q, k, v, ld, beta)


PIECES = 3
MESH = pl.DeviceIdType.MESH


def unpack_map(block):
    diag = block[W : W + 1, :W].astype(F32) + block[W + 1 : W + 2, :W].astype(F32)
    eye = iota((W, W), 0) == iota((W, W), 1)
    matrix = jnp.where(eye, diag, 0.0) - block[:W, :W].astype(F32)
    return jnp.concatenate([matrix, block[:W, W:].astype(F32)], axis=1), diag


def after(later, earlier):
    n = earlier.shape[1]
    out = mm4(later[:, :W], earlier)
    if n == 2 * W:
        return jnp.concatenate([out[:, :W], out[:, W:] + later[:, W:]], axis=1)
    return out + later[:, W:]


def carry_kernel(
    msg, base, carry, gate, out_gain, residual, hidden_gain, latent_gain, ow_hbm, lw_hbm, qw_hbm, ku_hbm,
    hidden_o, qp_o, latent_o,
    got, total, totals, states, state_in, partial, other, ow, lw, qw, ku,
    send_a, recv_a, send_b, recv_b, send_c, recv_c, send_p, recv_p, load_sem,
):
    heads = msg.shape[0]
    groups = totals.shape[0]
    here, core = lax.axis_index("seq"), lax.axis_index("head")
    mine, rank = here // heads, here % heads
    sibling = (here, 1 - core)

    def member(step):
        peer = (rank + step) % heads
        return peer, (mine * heads + peer, core)

    def cousin(step):
        peer = (mine + step) % groups
        return peer, (peer * heads + rank, core)

    loads = [
        pltpu.make_async_copy(src, dst, load_sem.at[i])
        for i, (src, dst) in enumerate(((ow_hbm, ow), (lw_hbm, lw), (qw_hbm, qw), (ku_hbm, ku)))
    ]

    barrier = pltpu.get_barrier_semaphore()
    for step in range(1, heads):
        pl.semaphore_signal(barrier, inc=1, device_id=member(step)[1], device_id_type=MESH)
    for step in range(1, groups):
        pl.semaphore_signal(barrier, inc=1, device_id=cousin(step)[1], device_id_type=MESH)
    pl.semaphore_signal(barrier, inc=1, device_id=sibling, device_id_type=MESH)
    pl.semaphore_wait(barrier, heads + groups - 1)

    def send_map(step):
        peer, device = member(step)
        return pltpu.make_async_remote_copy(
            src_ref=msg.at[peer], dst_ref=got.at[rank],
            send_sem=send_a.at[peer], recv_sem=recv_a.at[rank],
            device_id=device, device_id_type=MESH,
        )

    def take_map(step):
        peer, device = member(step)
        return pltpu.make_async_remote_copy(
            src_ref=msg.at[peer], dst_ref=got.at[peer],
            send_sem=send_a.at[peer], recv_sem=recv_a.at[peer],
            device_id=device, device_id_type=MESH,
        )

    for step in range(1, heads):
        send_map(step).start()
    for load in loads:
        load.start()
    got[rank] = msg[rank]
    for step in range(1, heads):
        take_map(step).wait_recv()

    maps, diags = [], []
    for i in range(heads):
        matrix, diag = unpack_map(got[i])
        maps.append(matrix)
        diags.append(diag)
    pairs = [after(maps[i + 1], maps[i]) for i in range(0, heads, 2)]
    quads = [after(pairs[i + 1], pairs[i]) for i in range(0, len(pairs), 2)]
    whole = after(quads[1], quads[0])
    diag = diags[0]
    for other_diag in diags[1:]:
        diag = diag * other_diag
    eye = iota((W, W), 0) == iota((W, W), 1)
    total[:W, :W] = (jnp.where(eye, diag, 0.0) - whole[:, :W]).astype(BF16)
    total[:W, W:] = whole[:, W:].astype(BF16)
    total[W:, :] = pack_diag(diag)

    def send_total(step):
        peer, device = cousin(step)
        return peer, pltpu.make_async_remote_copy(
            src_ref=total, dst_ref=totals.at[mine],
            send_sem=send_b.at[peer], recv_sem=recv_b.at[mine],
            device_id=device, device_id_type=MESH,
        )

    def take_total(step):
        peer, device = cousin(step)
        return peer, pltpu.make_async_remote_copy(
            src_ref=total, dst_ref=totals.at[peer],
            send_sem=send_b.at[peer], recv_sem=recv_b.at[peer],
            device_id=device, device_id_type=MESH,
        )

    for step in range(1, groups):
        peer, copy = send_total(step)
        pl.when(peer > mine)(copy.start)

    before = [None] * heads
    before[1] = maps[0]
    before[2] = pairs[0]
    before[4] = quads[0]
    before[3] = after(maps[2], pairs[0])
    before[5] = after(maps[4], quads[0])
    before[6] = after(pairs[2], quads[0])
    before[7] = after(maps[6], before[6])

    for step in range(1, groups):
        peer, copy = take_total(step)
        pl.when(peer < mine)(copy.wait_recv)

    eye_zero = jnp.concatenate([jnp.where(eye, 1.0, 0.0), jnp.zeros((W, W), F32)], axis=1)
    chain = [jnp.where(j < mine, unpack_map(totals[j])[0], eye_zero) for j in range(groups - 1)]
    while len(chain) > 1:
        joined = []
        for i in range(0, len(chain) - 1, 2):
            first = chain[i] if i else chain[i][:, W:]
            joined.append(after(chain[i + 1], first))
        if len(chain) % 2:
            joined.append(chain[-1])
        if joined[0].shape[1] == W:
            joined[0] = jnp.concatenate([jnp.zeros((W, W), F32), joined[0]], axis=1)
        chain = joined
    start = chain[0][:, W:]

    states[0] = start.astype(BF16)
    stacked = mm4(jnp.concatenate([b[:, :W] for b in before[1:]], axis=0), start)
    for i in range(1, heads):
        states[i] = (stacked[(i - 1) * W : i * W] + before[i][:, W:]).astype(BF16)

    def send_state(step):
        peer, device = member(step)
        return pltpu.make_async_remote_copy(
            src_ref=states.at[peer], dst_ref=state_in.at[rank],
            send_sem=send_c.at[peer], recv_sem=recv_c.at[rank],
            device_id=device, device_id_type=MESH,
        )

    def take_state(step):
        peer, device = member(step)
        return pltpu.make_async_remote_copy(
            src_ref=states.at[peer], dst_ref=state_in.at[peer],
            send_sem=send_c.at[peer], recv_sem=recv_c.at[peer],
            device_id=device, device_id_type=MESH,
        )

    for step in range(1, heads):
        send_state(step).start()
    state_in[rank] = states[rank]
    for step in range(1, heads):
        take_state(step).wait_recv()

    gated = []
    for h in range(heads):
        cols = slice(h * W, (h + 1) * W)
        raw = base[:, cols] + mm(carry[:, cols], state_in[h])
        raw = raw * lax.rsqrt(jnp.mean(raw * raw, axis=-1, keepdims=True) + EPS)
        logits = gate[:, cols].astype(F32)
        gated.append((raw * out_gain[...] / (1.0 + jnp.exp(-logits))).astype(BF16))
    gated = jnp.concatenate(gated, axis=1)

    loads[0].wait()
    width = partial.shape[2]

    def swap(p):
        return pltpu.make_async_remote_copy(
            src_ref=partial.at[p], dst_ref=other.at[p],
            send_sem=send_p.at[p], recv_sem=recv_p.at[p],
            device_id=sibling, device_id_type=MESH,
        )

    for p in range(PIECES):
        partial[p] = mm(gated, ow[:, p * width : (p + 1) * width])
        swap(p).start()
    squares = 0.0
    hidden = []
    for p in range(PIECES):
        cols = slice(p * width, (p + 1) * width)
        swap(p).wait_recv()
        summed = residual[:, cols].astype(F32) + (partial[p] + other[p])
        rounded = summed.astype(BF16)
        hidden_o[:, cols] = rounded
        rounded = rounded.astype(F32)
        squares = squares + jnp.sum(rounded * rounded, axis=-1, keepdims=True)
        hidden.append(rounded)
    scale = lax.rsqrt(squares / (PIECES * width) + EPS)
    normed = jnp.concatenate(hidden, axis=1) * scale * hidden_gain[...]
    normed = normed.astype(BF16)
    loads[1].wait()
    latent = mm(normed, lw[...])
    latent = latent * lax.rsqrt(jnp.mean(latent * latent, axis=-1, keepdims=True) + EPS)
    latent_o[...] = (latent * latent_gain[...]).astype(BF16)
    loads[2].wait()
    loads[3].wait()
    queries = mm(normed, qw[...]).astype(BF16)
    for h in range(heads):
        cols = slice(h * W, (h + 1) * W)
        qp_o[h] = (mm_nt(queries[:, cols], ku[:, cols]) * SCORE_SCALE).astype(BF16)

    for step in range(1, heads):
        send_map(step).wait_send()
        send_state(step).wait_send()
    for step in range(1, groups):
        peer, copy = send_total(step)
        pl.when(peer > mine)(copy.wait_send)
    for p in range(PIECES):
        swap(p).wait_send()


SCORE_SCALE = W ** (-0.5) * 1.4426950408889634


def carry_layer(msg, base, carry, gate, out_gain, residual, hidden_gain, latent_gain, ow, lw, qw, ku):
    heads = msg.shape[0]
    rows, width = residual.shape
    latent = lw.shape[1]
    groups = lax.axis_size("seq") // heads
    vm = pl.BlockSpec(memory_space=pltpu.VMEM)
    anywhere = pl.BlockSpec(memory_space=pl.ANY)
    dma = pltpu.SemaphoreType.DMA
    return pl.pallas_call(
        carry_kernel,
        out_shape=(
            jax.ShapeDtypeStruct((rows, width), BF16),
            jax.ShapeDtypeStruct((heads, rows, latent), BF16),
            jax.ShapeDtypeStruct((rows, latent), BF16),
        ),
        in_specs=[vm] * 8 + [anywhere] * 4,
        out_specs=(vm, vm, vm),
        scratch_shapes=[
            pltpu.VMEM(msg.shape, BF16),
            pltpu.VMEM(msg.shape[1:], BF16),
            pltpu.VMEM((groups,) + msg.shape[1:], BF16),
            pltpu.VMEM((heads, W, W), BF16),
            pltpu.VMEM((heads, W, W), BF16),
            pltpu.VMEM((PIECES, rows, width // PIECES), F32),
            pltpu.VMEM((PIECES, rows, width // PIECES), F32),
            pltpu.VMEM(ow.shape, BF16),
            pltpu.VMEM(lw.shape, BF16),
            pltpu.VMEM(qw.shape, BF16),
            pltpu.VMEM(ku.shape, BF16),
            dma((heads,)), dma((heads,)), dma((groups,)), dma((groups,)),
            dma((heads,)), dma((heads,)), dma((PIECES,)), dma((PIECES,)), dma((4,)),
        ],
        compiler_params=pltpu.CompilerParams(
            collective_id=0, has_side_effects=True, vmem_limit_bytes=56 * 2**20
        ),
        name="carry_layer",
    )(msg, base, carry, gate, out_gain, residual, hidden_gain, latent_gain, ow, lw, qw, ku)


KEYS = 512


def attend_kernel(qp_ref, vu_ref, latent_hbm, out_ref, latents, row_max, row_sum, accum, load_sem):
    heads, rows, latent = qp_ref.shape
    here = lax.axis_index("seq")
    lanes = W
    per = KEYS // rows

    def load(j):
        part = pl.ds(pl.multiple_of(j * KEYS, KEYS), KEYS)
        return pltpu.make_async_copy(latent_hbm.at[part], latents.at[part], load_sem.at[j])

    chunks = here // per + 1
    for j in range(latents.shape[0] // KEYS):
        pl.when(j < chunks)(load(j).start)
    row_max[...] = jnp.full(row_max.shape, -1e30, F32)
    row_sum[...] = jnp.zeros(row_sum.shape, F32)
    accum[...] = jnp.zeros(accum.shape, F32)
    block = GROUP * rows

    def chunk(j, masked):
        load(j).wait()
        keys = latents[pl.ds(pl.multiple_of(j * KEYS, KEYS), KEYS), :]
        for b in range(0, heads, GROUP):
            place = slice(b * rows, b * rows + block)
            scores = mm_nt(qp_ref[b : b + GROUP].reshape(block, latent), keys)
            if masked:
                query_pos = here * rows + iota((block, KEYS), 0) % rows
                key_pos = j * KEYS + iota((block, KEYS), 1)
                scores = jnp.where(key_pos <= query_pos, scores, -1e30)
            old = row_max[place, :]
            new = jnp.maximum(old, jnp.max(scores, axis=-1, keepdims=True))
            row_max[place, :] = new
            shrink = jnp.exp2(old - new)
            probs = [
                jnp.exp2(scores[:, c : c + lanes] - new) for c in range(0, KEYS, lanes)
            ]
            added = probs[0]
            for p in probs[1:]:
                added = added + p
            row_sum[place, :] = row_sum[place, :] * shrink + added
            mixed = mm(jnp.concatenate([p.astype(BF16) for p in probs], axis=1), keys)
            accum[place, :] = accum[place, :] * jnp.concatenate(
                [shrink] * (latent // lanes), axis=1
            ) + mixed

    def step(j, nothing):
        chunk(j, False)
        return nothing

    lax.fori_loop(0, chunks - 1, step, 0)
    chunk(chunks - 1, True)
    for h in range(heads):
        place = slice(h * rows, (h + 1) * rows)
        total = jnp.sum(row_sum[place, :], axis=-1, keepdims=True)
        mixed = accum[place, :] / total
        high, low = halves(mixed)
        cols = slice(h * W, (h + 1) * W)
        up = vu_ref[:, cols]
        out_ref[:, cols] = (mm(high, up) + mm(low, up)).astype(BF16)


GROUP = 4


def attend(qp, vu, latents):
    heads, rows, latent = qp.shape
    tokens = latents.shape[0]
    vm = pl.BlockSpec(memory_space=pltpu.VMEM)
    return pl.pallas_call(
        attend_kernel,
        out_shape=jax.ShapeDtypeStruct((rows, heads * W), BF16),
        in_specs=[vm, vm, pl.BlockSpec(memory_space=pl.ANY)],
        out_specs=vm,
        scratch_shapes=[
            pltpu.VMEM((tokens, latent), BF16),
            pltpu.VMEM((heads * rows, W), F32),
            pltpu.VMEM((heads * rows, W), F32),
            pltpu.VMEM((heads * rows, latent), F32),
            pltpu.SemaphoreType.DMA((tokens // KEYS,)),
        ],
        compiler_params=pltpu.CompilerParams(vmem_limit_bytes=56 * 2**20),
        name="attend",
    )(qp, vu, latents)


def body(
    residual, kda_query, kda_key, kda_value, log_decay, beta_logit, out_gate, out_gain, out_weight,
    hidden_gain, query_weight, latent_weight, latent_gain, key_up_weight, value_up_weight,
):
    msg, base, carry = delta_terms(kda_query, kda_key, kda_value, log_decay, beta_logit)
    hidden, qp, latent = carry_layer(
        msg, base, carry, out_gate, out_gain[None], residual, hidden_gain[None], latent_gain[None],
        out_weight, latent_weight, query_weight, key_up_weight,
    )
    latents = lax.all_gather(latent, "seq", axis=0, tiled=True)
    return hidden, attend(qp, value_up_weight, latents)


def solution(mesh):
    in_specs = (
        P("seq", None),
        P("seq", "head"),
        P("seq", "head"),
        P("seq", "head"),
        P("seq", "head"),
        P("seq", "head"),
        P("seq", "head"),
        P(),
        P("head", None),
        P(),
        P(None, "head"),
        P(),
        P(),
        P(None, "head"),
        P(None, "head"),
    )
    out_specs = (P("seq", None), P("seq", "head"))
    return jax.shard_map(body, mesh=mesh, in_specs=in_specs, out_specs=out_specs, check_vma=False)
```

time: 924 us -> 178 us (0.19)
  the two profiles are of different devices: /device:TPU:24 before, /device:TPU:31 now
where the time goes in v1:
time: 178 us
  waiting for transfers between devices  78.9 us (44%)
  Pallas kernels  75.8 us (43%)
  between operations  14.1 us (8%)
  local copies, waits for them, and re-layouts  9.12 us (5%)
    all_gather x1, waiting for transfers between devices, body(): latents = lax.all_gather(latent, 'seq', axis=0, tiled=True)  78.9 us
    pallas_call x1, Pallas kernels, carry_layer(): pl.pallas_call(carry_kernel, out_shape=(jax.ShapeDtypeStruct((rows, width...  39 us
    pallas_call x1, Pallas kernels, attend(): pl.pallas_call(attend_kernel, out_shape=jax.ShapeDtypeStruct((rows, heads...  29.1 us
    unnamed x18, local copies, waits for them, and re-layouts  7.81 us
    pallas_call x1, Pallas kernels, delta_terms(): pl.pallas_call(delta_kernel, out_shape=(jax.ShapeDtypeStruct((heads, W +...  7.8 us
  transfers between devices with their start and end apart: 1, of which 1 were waited for; matrix products, arithmetic and copies ran while one was open for 0% of the time, Pallas kernels for 0%

profile of v1, /device:TPU:31, one launch (start us, length us, event | category | flops | bytes accessed | tf_op | source)
XLA Modules:
  0.0 178.0 jit_solution(7168560261725281675)
XLA Ops:
  7.2 0.0 all-gather.2.cloned.1.call-start
  7.2 1.3 broadcast_in_dim.10.hidden_gain
  8.5 0.8 copy.17.beta_ref
  9.3 0.0 copy-start.2
  9.3 1.0 copy-done.2
  10.3 0.0 copy-start.4
  10.4 0.9 copy-done.4
  11.3 0.0 copy-start.5
  11.3 0.9 copy-done.5
  12.2 0.0 copy-start.6
  12.3 0.9 copy-done.6
  13.2 7.8 %delta_terms.1 = (bf16[8,144,256]{2,1,0:T(8,128)(2,1)S(1)}, f32[128,1024]{1,0:T(8,128)S(1)}, bf16[128,1024]{1,0:T(8,128)(2,1)S(1)}) custom-call(bf16[128,1024]{1,0:T(8,128)(2,1)S(1)} %copy-done.4, bf16[128,1024]{1,0:T(8,128)(2,1)S(1)} %copy-done.5, bf16[128,1024]{1,0:T(8,128)(2,1)S(1)} %copy-done.6, f32[128,1024]{1,0:T(8,128)S(1)} %copy-done.2, ...), custom_call_target="tpu_custom_call" | custom-call | tf_op jit(solution)/shard_map/delta_terms/pallas_call | solution.py:128
  21.0 0.0 copy-start
  21.0 0.8 copy-done
  21.8 0.0 copy-start.1
  21.8 0.8 copy-done.1
  22.6 0.0 copy-start.3
  22.6 0.7 copy-done.3
  23.3 39.0 %carry_layer.1 = (bf16[128,2304]{1,0:T(8,128)(2,1)}, bf16[8,128,512]{2,1,0:T(8,128)(2,1)}, bf16[128,512]{1,0:T(8,128)(2,1)}) custom-call(bf16[8,144,256]{2,1,0:T(8,128)(2,1)} %copy-done, f32[128,1024]{1,0:T(8,128)} %copy-done.1, bf16[128,1024]{1,0:T(8,128)(2,1)} %copy-done.3, bf16[128,1024]{1,0:T(8,128)(2,1)} %gate.1, f32[1,128]{1,0:T(1,128)} %bitcast.3, ...), custom_call_target="tpu_custom_call" | custom-call | tf_op jit(solution)/shard_map/carry_layer/pallas_call | solution.py:376
  62.3 0.0 all-gather.2.cloned.1.call-update
  62.3 78.9 %all-gather.2.cloned.1.call-done.latent_hbm = bf16[8192,512]{1,0:T(8,128)(2,1)} async-done(((bf16[128,512]{1,0:T(8,128)(2,1)}), bf16[8192,512]{1,0:T(8,128)(2,1)}) %all-gather.2.cloned.1.call-update) | async-done | bytes 8388624 | tf_op jit(solution)/shard_map/all_gather | solution.py:503
  141.2 0.0 copy-start.7
  141.2 29.1 %attend.1 = bf16[128,1024]{1,0:T(8,128)(2,1)} custom-call(bf16[8,128,512]{2,1,0:T(8,128)(2,1)} %get-tuple-element.12.qp_ref, bf16[512,1024]{1,0:T(8,128)(2,1)} %vu_ref.1, bf16[8192,512]{1,0:T(8,128)(2,1)} %all-gather.2.cloned.1.call-done.latent_hbm), custom_call_target="tpu_custom_call" | custom-call | tf_op jit(solution)/shard_map/attend/pallas_call | solution.py:477
  170.3 0.0 copy-done.7
  170.3 0.8 copy.19
Async XLA Ops:
  7.2 134.1 %all-gather.2.cloned.1.call-start = ((), (), s32[]{:S(2)}) async-start(), calls=%async_computation | async-start | bytes 8519680 | tf_op jit(solution)/shard_map/all_gather | solution.py:503
  9.3 1.0 copy-start.2
  10.3 0.9 copy-start.4
  11.3 0.9 copy-start.5
  12.2 0.9 copy-start.6
  21.0 0.8 copy-start
  21.8 0.8 copy-start.1
  22.6 0.7 copy-start.3
  141.2 29.1 %copy-start.7 = (bf16[128,2304]{1,0:T(8,128)(2,1)S(1)}, bf16[128,2304]{1,0:T(8,128)(2,1)}, u32[]{:S(2)}) copy-start(bf16[128,2304]{1,0:T(8,128)(2,1)} %get-tuple-element.16) | copy-start | bytes 1769476
Sparse Core Ops, SparseCore 0:
  62.4 78.7 all-gather.1

commit v2 on v1

--- a/solution.py
+++ b/solution.py
@@ -1,3 +1,4 @@
+import functools
 import jax
 import jax.numpy as jnp
 from jax import lax
@@ -404,59 +405,183 @@
     )(msg, base, carry, gate, out_gain, residual, hidden_gain, latent_gain, ow, lw, qw, ku)
 
 
-KEYS = 512
-
-
-def attend_kernel(qp_ref, vu_ref, latent_hbm, out_ref, latents, row_max, row_sum, accum, load_sem):
+RING = 4
+HALF = 64
+GROUP = 4
+
+
+def attend_kernel(
+    qp_ref, vu_ref, latent_ref, out_ref, lat, row_max, row_sum, accum,
+    send_y, recv_y, send_b, recv_b, send_a, recv_a, send_s, recv_s,
+):
     heads, rows, latent = qp_ref.shape
-    here = lax.axis_index("seq")
-    lanes = W
-    per = KEYS // rows
-
-    def load(j):
-        part = pl.ds(pl.multiple_of(j * KEYS, KEYS), KEYS)
-        return pltpu.make_async_copy(latent_hbm.at[part], latents.at[part], load_sem.at[j])
-
-    chunks = here // per + 1
-    for j in range(latents.shape[0] // KEYS):
-        pl.when(j < chunks)(load(j).start)
+    here, core = lax.axis_index("seq"), lax.axis_index("head")
+    y, x, z = here // (RING * RING), (here // RING) % RING, here % RING
+    mine_a = jnp.where(core == 0, z, x)
+    mine_b = jnp.where(core == 0, x, z)
+    piece_rows = RING * HALF
+
+    def device(to_y, to_a, to_b):
+        inside = jnp.where(core == 0, to_b * RING + to_a, to_a * RING + to_b)
+        return (to_y * RING * RING + inside, core)
+
+    sibling = (here, 1 - core)
+
+    def other(coordinate, step):
+        return (coordinate + step) % RING
+
+    barrier = pltpu.get_barrier_semaphore()
+    for step in range(1, RING):
+        for peer in (
+            device(other(y, step), mine_a, mine_b),
+            device(y, other(mine_a, step), mine_b),
+            device(y, mine_a, other(mine_b, step)),
+        ):
+            pl.semaphore_signal(barrier, inc=1, device_id=peer, device_id_type=MESH)
+    pl.semaphore_signal(barrier, inc=1, device_id=sibling, device_id_type=MESH)
+    pl.semaphore_wait(barrier, 3 * (RING - 1) + 1)
+
+    def remote(place, peer, send, recv):
+        return pltpu.make_async_remote_copy(
+            src_ref=place, dst_ref=place, send_sem=send, recv_sem=recv,
+            device_id=peer, device_id_type=MESH,
+        )
+
+    def over_y(step):
+        peer = device(other(y, step), mine_a, mine_b)
+        return other(y, step), remote(
+            lat.at[core, y, mine_a, mine_b], peer, send_y.at[step], recv_y.at[y]
+        )
+
+    def from_y(at):
+        return remote(
+            lat.at[core, at, mine_a, mine_b], sibling, send_y.at[0], recv_y.at[at]
+        )
+
+    def over_b(at, step):
+        return remote(
+            lat.at[core, at, mine_a, mine_b], device(y, mine_a, other(mine_b, step)),
+            send_b.at[at, step], recv_b.at[at, RING - step],
+        )
+
+    def from_b(at, step):
+        return remote(
+            lat.at[core, at, mine_a, other(mine_b, step)], sibling,
+            send_b.at[at, 0], recv_b.at[at, step],
+        )
+
+    def over_a(at, step):
+        return remote(
+            lat.at[core, at, mine_a], device(y, other(mine_a, step), mine_b),
+            send_a.at[at, step], recv_a.at[at, RING - step],
+        )
+
+    def from_a(at, step):
+        return remote(
+            lat.at[core, at, other(mine_a, step)], sibling, send_a.at[at, 0], recv_a.at[at, step]
+        )
+
+    def to_sibling(at, step):
+        return remote(
+            lat.at[core, at, other(mine_a, step)], sibling, send_s.at[at, step], recv_s.at[at, step]
+        )
+
+    def from_sibling(at, step):
+        return remote(
+            lat.at[1 - core, at, other(mine_b, step)], sibling,
+            send_s.at[at, step], recv_s.at[at, step],
+        )
+
+    lat[core, y, mine_a, mine_b] = latent_ref[pl.ds(pl.multiple_of(core * HALF, HALF), HALF), :]
+    for step in range(1, RING):
+        peer_y, copy = over_y(step)
+        pl.when(peer_y > y)(copy.start)
+
+    def spread(at):
+        for step in range(1, RING):
+            over_b(at, step).start()
+
+    def complete(at):
+        for step in range(1, RING):
+            from_b(at, step).wait_recv()
+        for step in (1, 3, 2):
+            over_a(at, step).start()
+        to_sibling(at, 0).start()
+
+    spread(y)
+    for at in range(RING - 1):
+
+        @pl.when(at < y)
+        def _():
+            from_y(at).wait_recv()
+            spread(at)
+
     row_max[...] = jnp.full(row_max.shape, -1e30, F32)
     row_sum[...] = jnp.zeros(row_sum.shape, F32)
     accum[...] = jnp.zeros(accum.shape, F32)
     block = GROUP * rows
 
-    def chunk(j, masked):
-        load(j).wait()
-        keys = latents[pl.ds(pl.multiple_of(j * KEYS, KEYS), KEYS), :]
+    complete(y)
+    for at in range(RING - 1):
+        pl.when(at < y)(functools.partial(complete, at))
+
+    def work(at, step, masked):
+        first_a, second_a = other(z, step), other(x, step)
+        keys = (
+            lat[0, at, first_a].reshape(piece_rows, latent),
+            lat[1, at, second_a].reshape(piece_rows, latent),
+        )
         for b in range(0, heads, GROUP):
             place = slice(b * rows, b * rows + block)
-            scores = mm_nt(qp_ref[b : b + GROUP].reshape(block, latent), keys)
+            queries = qp_ref[b : b + GROUP].reshape(block, latent)
+            scores = [mm_nt(queries, part) for part in keys]
             if masked:
-                query_pos = here * rows + iota((block, KEYS), 0) % rows
-                key_pos = j * KEYS + iota((block, KEYS), 1)
-                scores = jnp.where(key_pos <= query_pos, scores, -1e30)
+                query_pos = here * rows + iota((block, piece_rows), 0) % rows
+                column = iota((block, piece_rows), 1)
+                slot, inner = column // HALF, column % HALF
+                first_pos = (at * RING * RING + slot * RING + first_a) * rows + inner
+                second_pos = (at * RING * RING + second_a * RING + slot) * rows + HALF + inner
+                scores = [
+                    jnp.where(pos <= query_pos, part, -2e30)
+                    for pos, part in zip((first_pos, second_pos), scores)
+                ]
             old = row_max[place, :]
-            new = jnp.maximum(old, jnp.max(scores, axis=-1, keepdims=True))
+            top = jnp.maximum(scores[0], scores[1])
+            new = jnp.maximum(old, jnp.max(top, axis=-1, keepdims=True))
             row_max[place, :] = new
             shrink = jnp.exp2(old - new)
-            probs = [
-                jnp.exp2(scores[:, c : c + lanes] - new) for c in range(0, KEYS, lanes)
-            ]
-            added = probs[0]
-            for p in probs[1:]:
-                added = added + p
-            row_sum[place, :] = row_sum[place, :] * shrink + added
-            mixed = mm(jnp.concatenate([p.astype(BF16) for p in probs], axis=1), keys)
-            accum[place, :] = accum[place, :] * jnp.concatenate(
-                [shrink] * (latent // lanes), axis=1
-            ) + mixed
-
-    def step(j, nothing):
-        chunk(j, False)
-        return nothing
-
-    lax.fori_loop(0, chunks - 1, step, 0)
-    chunk(chunks - 1, True)
+            added = row_sum[place, :] * shrink
+            mixed = accum[place, :] * jnp.concatenate([shrink] * (latent // W), axis=1)
+            for part, key in zip(scores, keys):
+                probs = [jnp.exp2(part[:, c : c + W] - new) for c in range(0, piece_rows, W)]
+                for p in probs:
+                    added = added + p
+                mixed = mixed + mm(jnp.concatenate([p.astype(BF16) for p in probs], axis=1), key)
+            row_sum[place, :] = added
+            accum[place, :] = mixed
+
+    def near(at, masked):
+        from_sibling(at, 0).wait_recv()
+        work(at, 0, masked)
+
+    def far(at, step, masked):
+        from_a(at, step).wait_recv()
+        to_sibling(at, step).start()
+        from_sibling(at, step).wait_recv()
+        work(at, step, masked)
+
+    def loop(lower, upper, visit):
+        lax.fori_loop(lower, upper, lambda i, nothing: (visit(i), nothing)[1], 0)
+
+    near(y, True)
+    loop(0, y, lambda at: near(at, False))
+
+    def round_of(step):
+        far(y, step, True)
+        loop(0, y, lambda at: far(at, step, False))
+
+    loop(1, RING, round_of)
+
     for h in range(heads):
         place = slice(h * rows, (h + 1) * rows)
         total = jnp.sum(row_sum[place, :], axis=-1, keepdims=True)
@@ -466,29 +591,42 @@
         up = vu_ref[:, cols]
         out_ref[:, cols] = (mm(high, up) + mm(low, up)).astype(BF16)
 
-
-GROUP = 4
-
-
-def attend(qp, vu, latents):
-    heads, rows, latent = qp.shape
-    tokens = latents.shape[0]
+    for step in range(1, RING):
+        peer_y, copy = over_y(step)
+        pl.when(peer_y > y)(copy.wait_send)
+
+    def drain(at):
+        for step in range(1, RING):
+            over_b(at, step).wait_send()
+            over_a(at, step).wait_send()
+        for step in range(RING):
+            to_sibling(at, step).wait_send()
+
+    loop(0, y + 1, drain)
+
+
+def attend(qp, vu, latent):
+    heads, rows, width = qp.shape
     vm = pl.BlockSpec(memory_space=pltpu.VMEM)
+    dma = pltpu.SemaphoreType.DMA
+    ring = (RING, RING)
     return pl.pallas_call(
         attend_kernel,
         out_shape=jax.ShapeDtypeStruct((rows, heads * W), BF16),
-        in_specs=[vm, vm, pl.BlockSpec(memory_space=pl.ANY)],
+        in_specs=[vm, vm, vm],
         out_specs=vm,
         scratch_shapes=[
-            pltpu.VMEM((tokens, latent), BF16),
+            pltpu.VMEM((2, RING, RING, RING, HALF, width), BF16),
             pltpu.VMEM((heads * rows, W), F32),
             pltpu.VMEM((heads * rows, W), F32),
-            pltpu.VMEM((heads * rows, latent), F32),
-            pltpu.SemaphoreType.DMA((tokens // KEYS,)),
+            pltpu.VMEM((heads * rows, width), F32),
+            dma((RING,)), dma((RING,)), dma(ring), dma(ring), dma(ring), dma(ring), dma(ring), dma(ring),
         ],
-        compiler_params=pltpu.CompilerParams(vmem_limit_bytes=56 * 2**20),
+        compiler_params=pltpu.CompilerParams(
+            collective_id=1, has_side_effects=True, vmem_limit_bytes=56 * 2**20
+        ),
         name="attend",
-    )(qp, vu, latents)
+    )(qp, vu, latent)
 
 
 def body(
@@ -500,8 +638,7 @@
         msg, base, carry, out_gate, out_gain[None], residual, hidden_gain[None], latent_gain[None],
         out_weight, latent_weight, query_weight, key_up_weight,
     )
-    latents = lax.all_gather(latent, "seq", axis=0, tiled=True)
-    return hidden, attend(qp, value_up_weight, latents)
+    return hidden, attend(qp, value_up_weight, latent)
 
 
 def solution(mesh):

time: 178 us -> 123 us (0.69)
  the two profiles are of different devices: /device:TPU:31 before, /device:TPU:24 now
where the time goes in v2:
time: 123 us; the launch traced here: 122 us
  Pallas kernels  110 us (89%)
  local copies, waits for them, and re-layouts  11.9 us (10%)
    pallas_call x1, Pallas kernels, attend(): pl.pallas_call(attend_kernel, out_shape=jax.ShapeDtypeStruct((rows, heads...  65.2 us
    pallas_call x1, Pallas kernels, carry_layer(): pl.pallas_call(carry_kernel, out_shape=(jax.ShapeDtypeStruct((rows, width...  36.6 us
    unnamed x17, local copies, waits for them, and re-layouts  10.6 us
    pallas_call x1, Pallas kernels, delta_terms(): pl.pallas_call(delta_kernel, out_shape=(jax.ShapeDtypeStruct((heads, W +...  7.8 us

profile of v2, /device:TPU:24, one launch (start us, length us, event | category | flops | bytes accessed | tf_op | source)
XLA Modules:
  0.0 122.1 jit_solution(17724182103784347805)
XLA Ops:
  0.6 1.3 %broadcast_in_dim.10.hidden_gain = f32[1,2304]{1,0:T(1,128)} reshape(f32[2304]{0:T(1024)} %param.24) | data formatting | bytes 18432 | tf_op jit(solution)/shard_map/broadcast_in_dim | solution.py:638
  1.9 0.8 copy.17.beta_ref
  2.7 0.0 copy-start.2
  2.7 1.0 copy-done.2
  3.8 0.0 copy-start.4
  3.8 0.9 copy-done.4
  4.7 0.0 copy-start.5
  4.7 0.9 copy-done.5
  5.7 0.0 copy-start.6
  5.7 0.9 copy-done.6
  6.6 7.8 %delta_terms.1 = (bf16[8,144,256]{2,1,0:T(8,128)(2,1)S(1)}, f32[128,1024]{1,0:T(8,128)S(1)}, bf16[128,1024]{1,0:T(8,128)(2,1)S(1)}) custom-call(bf16[128,1024]{1,0:T(8,128)(2,1)S(1)} %copy-done.4, bf16[128,1024]{1,0:T(8,128)(2,1)S(1)} %copy-done.5, bf16[128,1024]{1,0:T(8,128)(2,1)S(1)} %copy-done.6, f32[128,1024]{1,0:T(8,128)S(1)} %copy-done.2, ...), custom_call_target="tpu_custom_call" | custom-call | tf_op jit(solution)/shard_map/delta_terms/pallas_call | solution.py:129
  14.4 0.0 copy-start
  14.4 0.8 copy-done
  15.2 0.0 copy-start.1
  15.2 0.8 copy-done.1
  16.0 0.0 copy-start.3
  16.0 0.7 copy-done.3
  16.8 36.6 %carry_layer.1 = (bf16[128,2304]{1,0:T(8,128)(2,1)}, bf16[8,128,512]{2,1,0:T(8,128)(2,1)}, bf16[128,512]{1,0:T(8,128)(2,1)}) custom-call(bf16[8,144,256]{2,1,0:T(8,128)(2,1)} %copy-done, f32[128,1024]{1,0:T(8,128)} %copy-done.1, bf16[128,1024]{1,0:T(8,128)(2,1)} %copy-done.3, bf16[128,1024]{1,0:T(8,128)(2,1)} %gate.1, f32[1,128]{1,0:T(1,128)} %bitcast.3, ...), custom_call_target="tpu_custom_call" | custom-call | tf_op jit(solution)/shard_map/carry_layer/pallas_call | solution.py:377
  53.3 65.2 %attend.1 = bf16[128,1024]{1,0:T(8,128)(2,1)} custom-call(bf16[8,128,512]{2,1,0:T(8,128)(2,1)} %get-tuple-element.12.qp_ref, bf16[512,1024]{1,0:T(8,128)(2,1)} %vu_ref.1, bf16[128,512]{1,0:T(8,128)(2,1)} %get-tuple-element.13.latent_ref), custom_call_target="tpu_custom_call" | custom-call | tf_op jit(solution)/shard_map/attend/pallas_call | solution.py:613
  118.6 1.9 %copy.20 = bf16[128,2304]{1,0:T(8,128)(2,1)} copy(bf16[128,2304]{1,0:T(8,128)(2,1)} %get-tuple-element.16) | data formatting | bytes 1179648
  120.5 1.7 %copy.21 = bf16[128,1024]{1,0:T(8,128)(2,1)} copy(bf16[128,1024]{1,0:T(8,128)(2,1)} %attend.1) | data formatting | bytes 524288
Async XLA Ops:
  2.7 1.0 copy-start.2
  3.8 0.9 copy-start.4
  4.7 0.9 copy-start.5
  5.7 0.9 copy-start.6
  14.4 0.8 copy-start
  15.2 0.8 copy-start.1
  16.0 0.7 copy-start.3

commit v3 on v1

v3 whole, which is shorter than its diff:
```python
import functools
import jax
import jax.numpy as jnp
from jax import lax
from jax.sharding import PartitionSpec as P
from jax.experimental import pallas as pl
from jax.experimental.pallas import tpu as pltpu

F32 = jnp.float32
BF16 = jnp.bfloat16
W = 128
EPS = 1e-06


def halves(x):
    high = x.astype(BF16)
    return high, (x - high.astype(F32)).astype(BF16)


def mm(a, b):
    return jnp.dot(a, b, preferred_element_type=F32)


def mm_nt(a, b):
    return lax.dot_general(a, b, (((1,), (1,)), ((), ())), preferred_element_type=F32)


def wide(x):
    high, low = halves(x)
    return jnp.concatenate([high, low], axis=1)


def mm4(a, b):
    n = b.shape[1]
    right = wide(b)
    out = mm(wide(a), jnp.concatenate([right, right], axis=0))
    return out[:, :n] + out[:, n:]


def mm4_nt(a, b):
    n = b.shape[0]
    high, low = halves(b)
    right = jnp.concatenate(
        [jnp.concatenate([high, high], axis=1), jnp.concatenate([low, low], axis=1)], axis=0
    )
    out = mm_nt(wide(a), right)
    return out[:, :n] + out[:, n:]


def iota(shape, axis):
    return lax.broadcasted_iota(jnp.int32, shape, axis)


PIECES = 3
MESH = pl.DeviceIdType.MESH
SCORE_SCALE = W ** (-0.5) * 1.4426950408889634
RING = 4
PART = 32
GROUP = 4


def pack_diag(closing):
    high, rest = halves(closing)
    r = iota((16, W), 0)
    block = jnp.where(r == 0, high.astype(F32), jnp.where(r == 1, rest.astype(F32), 0.0))
    return jnp.concatenate([block, jnp.zeros((16, W), F32)], axis=1).astype(BF16)


def unpack_map(block):
    diag = block[W : W + 1, :W].astype(F32) + block[W + 1 : W + 2, :W].astype(F32)
    eye = iota((W, W), 0) == iota((W, W), 1)
    matrix = jnp.where(eye, diag, 0.0) - block[:W, :W].astype(F32)
    return jnp.concatenate([matrix, block[:W, W:].astype(F32)], axis=1), diag


def after(later, earlier):
    n = earlier.shape[1]
    out = mm4(later[:, :W], earlier)
    if n == 2 * W:
        return jnp.concatenate([out[:, :W], out[:, W:] + later[:, W:]], axis=1)
    return out + later[:, W:]


def delta_part(q_ref, k_ref, v_ref, ld_ref, beta_ref, msg_ref, base_ref, carry_ref, sent):
    rows = q_ref.shape[0]
    heads = q_ref.shape[1] // W
    ti, si = iota((rows, rows), 0), iota((rows, rows), 1)
    ones = jnp.where(si <= ti, 1.0, 0.0).astype(BF16)
    strict = si < ti
    through = si <= ti
    eye = jnp.where(si == ti, 1.0, 0.0)
    rates = (1.0 / (1.0 + jnp.exp(-beta_ref[...]))).T

    def stage_one(h):
        cols = slice(h * W, (h + 1) * W)
        ld = ld_ref[:, cols]
        high, rest = halves(ld)
        low = (ld - high.astype(F32) - rest.astype(F32)).astype(BF16)
        cum = mm(ones, high) + (mm(ones, rest) + mm(ones, low))
        mid = cum[rows // 2 - 1 : rows // 2, :]
        end = cum[rows - 1 : rows, :]
        key = k_ref[:, cols].astype(F32)
        key = key * lax.rsqrt(jnp.sum(key * key, axis=-1, keepdims=True) + EPS)
        query = q_ref[:, cols].astype(F32)
        query = query * lax.rsqrt(jnp.sum(query * query, axis=-1, keepdims=True) + EPS)
        forward = jnp.exp(cum - mid)
        mixed = mm4_nt(
            jnp.concatenate([key * forward, query * forward], axis=0), key * jnp.exp(mid - cum)
        )
        rate = rates[:, h : h + 1]
        lower = jnp.where(strict, mixed[:rows], 0.0) * rate
        mix = jnp.where(through, mixed[rows:], 0.0)
        growth = jnp.exp(cum)
        right = jnp.concatenate(
            [rate * v_ref[:, cols].astype(F32), rate * (key * growth)], axis=1
        )
        tail = (key * jnp.exp(end - cum)).T
        return lower, mix, right, tail, query * growth, jnp.exp(end)

    def invert(lowers):
        level = jnp.logical_and((ti // 2) == (si // 2), strict)
        found = [eye - jnp.where(level, low, 0.0) for low in lowers]
        size = 2
        while size < rows:
            level = jnp.logical_and((ti // (2 * size)) == (si // (2 * size)),
                                    (ti // size) > (si // size))
            inner = [mm4(jnp.where(level, low, 0.0), x) for low, x in zip(lowers, found)]
            found = [x - mm4(x, y) for x, y in zip(found, inner)]
            size *= 2
        return found

    group = 4
    for start in range(0, heads, group):
        made = [stage_one(h) for h in range(start, start + group)]
        inverses = invert([m[0] for m in made])
        for h in range(start, start + group):
            _, mix, right, tail, query, closing = made[h - start]
            solved = mm4(inverses[h - start], right)
            state = mm4(tail, solved)
            out = mm4(mix, solved)
            cols = slice(h * W, (h + 1) * W)
            base_ref[:, cols] = out[:, :W]
            carry_ref[:, cols] = (query - out[:, W:]).astype(BF16)
            msg_ref[h, :W, :W] = state[:, W:].astype(BF16)
            msg_ref[h, :W, W:] = state[:, :W].astype(BF16)
            msg_ref[h, W:, :] = pack_diag(closing)
        sent(start, start + group)


def layer_kernel(
    q_hbm, k_hbm, v_hbm, ld_hbm, beta_hbm, gate_hbm, residual_hbm, out_gain_hbm, hidden_gain_hbm,
    latent_gain_hbm, ow_hbm, lw_hbm, qw_hbm, ku_hbm, vu_hbm,
    hidden_o, out_ref,
    q_in, k_in, v_in, ld_in, beta_in, gate, residual, out_gain, hidden_gain, latent_gain, ow, lw, qw, ku, vu_ref,
    msg, base, carry, got, total, totals, states, state_in, partial, other,
    qp_ref, lat_a, lat_b, row_max, row_sum, accum,
    load_sem, send_a, recv_a, send_b, recv_b, send_c, recv_c, send_p, recv_p,
    sa1, ra1, sa2, ra2, sa3, ra3, sb1, rb1, sb2, rb2, sb3, rb3, swap_a, got_a, swap_b, got_b,
):
    heads = msg.shape[0]
    groups = totals.shape[0]
    rows, latent = residual.shape[0], lw.shape[1]
    here, core = lax.axis_index("seq"), lax.axis_index("head")
    mine, rank = here // heads, here % heads
    y, x, z = here // (RING * RING), (here // RING) % RING, here % RING
    line = RING * PART
    sibling = (here, 1 - core)

    def device(to_y, to_x, to_z):
        return (to_y * RING * RING + to_x * RING + to_z, core)

    def turn(coordinate, step):
        return (coordinate + step) % RING

    def member(step):
        peer = (rank + step) % heads
        return peer, (mine * heads + peer, core)

    def cousin(step):
        peer = (mine + step) % groups
        return peer, (peer * heads + rank, core)

    barrier = pltpu.get_barrier_semaphore()
    for step in range(1, heads):
        pl.semaphore_signal(barrier, inc=1, device_id=member(step)[1], device_id_type=MESH)
    for step in range(1, groups):
        pl.semaphore_signal(barrier, inc=1, device_id=cousin(step)[1], device_id_type=MESH)
    pl.semaphore_signal(barrier, inc=1, device_id=sibling, device_id_type=MESH)
    pl.semaphore_signal(barrier, inc=1, device_id=device(y, RING - 1 - x, z), device_id_type=MESH)

    pairs = (
        (k_hbm, k_in), (ld_hbm, ld_in), (q_hbm, q_in), (v_hbm, v_in), (beta_hbm, beta_in), (gate_hbm, gate),
        (residual_hbm, residual), (out_gain_hbm, out_gain), (hidden_gain_hbm, hidden_gain),
        (latent_gain_hbm, latent_gain), (ow_hbm, ow), (lw_hbm, lw), (qw_hbm, qw), (ku_hbm, ku), (vu_hbm, vu_ref),
    )
    loads = [pltpu.make_async_copy(src, dst, load_sem.at[i]) for i, (src, dst) in enumerate(pairs)]
    for load in loads:
        load.start()
    for load in loads[:5]:
        load.wait()

    def map_to(peer):
        return pltpu.make_async_remote_copy(
            src_ref=msg.at[peer], dst_ref=got.at[rank],
            send_sem=send_a.at[peer], recv_sem=recv_a.at[rank],
            device_id=(mine * heads + peer, core), device_id_type=MESH,
        )

    def map_from(peer):
        return pltpu.make_async_remote_copy(
            src_ref=msg.at[peer], dst_ref=got.at[peer],
            send_sem=send_a.at[peer], recv_sem=recv_a.at[peer],
            device_id=(mine * heads + peer, core), device_id_type=MESH,
        )

    def sent(begin, end):
        if begin == 0:
            pl.semaphore_wait(barrier, heads + groups)
        for peer in range(begin, end):
            pl.when(peer != rank)(map_to(peer).start)

    delta_part(q_in, k_in, v_in, ld_in, beta_in, msg, base, carry, sent)
    got[rank] = msg[rank]
    for step in range(1, heads):
        map_from(member(step)[0]).wait_recv()

    maps, diags = [], []
    for i in range(heads):
        matrix, diag = unpack_map(got[i])
        maps.append(matrix)
        diags.append(diag)
    pairs = [after(maps[i + 1], maps[i]) for i in range(0, heads, 2)]
    quads = [after(pairs[i + 1], pairs[i]) for i in range(0, len(pairs), 2)]
    whole = after(quads[1], quads[0])
    diag = diags[0]
    for other_diag in diags[1:]:
        diag = diag * other_diag
    eye = iota((W, W), 0) == iota((W, W), 1)
    total[:W, :W] = (jnp.where(eye, diag, 0.0) - whole[:, :W]).astype(BF16)
    total[:W, W:] = whole[:, W:].astype(BF16)
    total[W:, :] = pack_diag(diag)

    def send_total(step):
        peer, device = cousin(step)
        return peer, pltpu.make_async_remote_copy(
            src_ref=total, dst_ref=totals.at[mine],
            send_sem=send_b.at[peer], recv_sem=recv_b.at[mine],
            device_id=device, device_id_type=MESH,
        )

    def take_total(step):
        peer, device = cousin(step)
        return peer, pltpu.make_async_remote_copy(
            src_ref=total, dst_ref=totals.at[peer],
            send_sem=send_b.at[peer], recv_sem=recv_b.at[peer],
            device_id=device, device_id_type=MESH,
        )

    for step in range(1, groups):
        peer, copy = send_total(step)
        pl.when(peer > mine)(copy.start)

    before = [None] * heads
    before[1] = maps[0]
    before[2] = pairs[0]
    before[4] = quads[0]
    before[3] = after(maps[2], pairs[0])
    before[5] = after(maps[4], quads[0])
    before[6] = after(pairs[2], quads[0])
    before[7] = after(maps[6], before[6])

    for step in range(1, groups):
        peer, copy = take_total(step)
        pl.when(peer < mine)(copy.wait_recv)

    eye_zero = jnp.concatenate([jnp.where(eye, 1.0, 0.0), jnp.zeros((W, W), F32)], axis=1)
    chain = [jnp.where(j < mine, unpack_map(totals[j])[0], eye_zero) for j in range(groups - 1)]
    while len(chain) > 1:
        joined = []
        for i in range(0, len(chain) - 1, 2):
            first = chain[i] if i else chain[i][:, W:]
            joined.append(after(chain[i + 1], first))
        if len(chain) % 2:
            joined.append(chain[-1])
        if joined[0].shape[1] == W:
            joined[0] = jnp.concatenate([jnp.zeros((W, W), F32), joined[0]], axis=1)
        chain = joined
    start = chain[0][:, W:]

    states[0] = start.astype(BF16)
    stacked = mm4(jnp.concatenate([b[:, :W] for b in before[1:]], axis=0), start)
    for i in range(1, heads):
        states[i] = (stacked[(i - 1) * W : i * W] + before[i][:, W:]).astype(BF16)

    def send_state(step):
        peer, device = member(step)
        return pltpu.make_async_remote_copy(
            src_ref=states.at[peer], dst_ref=state_in.at[rank],
            send_sem=send_c.at[peer], recv_sem=recv_c.at[rank],
            device_id=device, device_id_type=MESH,
        )

    def take_state(step):
        peer, device = member(step)
        return pltpu.make_async_remote_copy(
            src_ref=states.at[peer], dst_ref=state_in.at[peer],
            send_sem=send_c.at[peer], recv_sem=recv_c.at[peer],
            device_id=device, device_id_type=MESH,
        )

    for step in range(1, heads):
        send_state(step).start()
    state_in[rank] = states[rank]
    for step in range(1, heads):
        take_state(step).wait_recv()

    for load in loads[5:10]:
        load.wait()
    gated = []
    for h in range(heads):
        cols = slice(h * W, (h + 1) * W)
        raw = base[:, cols] + mm(carry[:, cols], state_in[h])
        raw = raw * lax.rsqrt(jnp.mean(raw * raw, axis=-1, keepdims=True) + EPS)
        logits = gate[:, cols].astype(F32)
        gated.append((raw * out_gain[...] / (1.0 + jnp.exp(-logits))).astype(BF16))
    gated = jnp.concatenate(gated, axis=1)

    loads[10].wait()
    width = partial.shape[2]

    def swap(p):
        return pltpu.make_async_remote_copy(
            src_ref=partial.at[p], dst_ref=other.at[p],
            send_sem=send_p.at[p], recv_sem=recv_p.at[p],
            device_id=sibling, device_id_type=MESH,
        )

    for p in range(PIECES):
        partial[p] = mm(gated, ow[:, p * width : (p + 1) * width])
        swap(p).start()
    squares = 0.0
    hidden = []
    for p in range(PIECES):
        cols = slice(p * width, (p + 1) * width)
        swap(p).wait_recv()
        summed = residual[:, cols].astype(F32) + (partial[p] + other[p])
        rounded = summed.astype(BF16)
        hidden_o[:, cols] = rounded
        rounded = rounded.astype(F32)
        squares = squares + jnp.sum(rounded * rounded, axis=-1, keepdims=True)
        hidden.append(rounded)
    scale = lax.rsqrt(squares / (PIECES * width) + EPS)
    gain = jnp.concatenate([hidden_gain[i : i + 1] for i in range(hidden_gain.shape[0])], axis=1)
    normed = jnp.concatenate(hidden, axis=1) * scale * gain
    normed = normed.astype(BF16)
    loads[11].wait()
    raw = mm(normed, lw[...])
    raw = raw * lax.rsqrt(jnp.mean(raw * raw, axis=-1, keepdims=True) + EPS)
    raw = (raw * latent_gain[...]).astype(BF16)

    def place_parts(which):
        first = which * 2 * PART
        lat_a[core, y, x, z] = raw[first : first + PART]
        lat_b[core, y, z, x] = raw[first + PART : first + 2 * PART]

    for which in range(2):
        pl.when(core == which)(functools.partial(place_parts, which))
    def remote(place, peer, send, recv):
        return pltpu.make_async_remote_copy(
            src_ref=place, dst_ref=place, send_sem=send, recv_sem=recv,
            device_id=peer, device_id_type=MESH,
        )

    def a_over_z(step):
        return remote(lat_a.at[core, y, x, z], device(y, x, turn(z, step)), sa1.at[step], ra1.at[RING - step])

    def a_from_z(step):
        return remote(lat_a.at[core, y, x, turn(z, step)], sibling, sa1.at[0], ra1.at[step])

    def a_over_x(step):
        return remote(lat_a.at[core, y, x], device(y, turn(x, step), z), sa2.at[step], ra2.at[RING - step])

    def a_from_x(step):
        return remote(lat_a.at[core, y, turn(x, step)], sibling, sa2.at[0], ra2.at[step])

    def a_over_y(to, step):
        return remote(
            lat_a.at[core, y, turn(x, step)], device(to, x, z), sa3.at[to, step], ra3.at[y, step]
        )

    def a_from_y(at, step):
        return remote(lat_a.at[core, at, turn(x, step)], sibling, sa3.at[at, 0], ra3.at[at, step])

    def b_over_y(to):
        return remote(lat_b.at[core, y, z, x], device(to, x, z), sb1.at[to], rb1.at[y])

    def b_from_y(at):
        return remote(lat_b.at[core, at, z, x], sibling, sb1.at[at], rb1.at[at])

    def b_over_x(at, step):
        return remote(
            lat_b.at[core, at, z, x], device(y, turn(x, step), z), sb2.at[at, step], rb2.at[at, RING - step]
        )

    def b_from_x(at, step):
        return remote(lat_b.at[core, at, z, turn(x, step)], sibling, sb2.at[at, 0], rb2.at[at, step])

    def b_over_z(at, step):
        return remote(
            lat_b.at[core, at, z], device(y, x, turn(z, step)), sb3.at[at, step], rb3.at[at, RING - step]
        )

    def b_from_z(at, step):
        return remote(lat_b.at[core, at, turn(z, step)], sibling, sb3.at[at, 0], rb3.at[at, step])

    def give_a(at, step):
        return remote(lat_a.at[core, at, turn(x, step)], sibling, swap_a.at[at, step], got_a.at[at, step])

    def take_a(at, step):
        return remote(lat_a.at[1 - core, at, turn(x, step)], sibling, swap_a.at[at, step], got_a.at[at, step])

    def give_b(at, step):
        return remote(lat_b.at[core, at, turn(z, step)], sibling, swap_b.at[at, step], got_b.at[at, step])

    def take_b(at, step):
        return remote(lat_b.at[1 - core, at, turn(z, step)], sibling, swap_b.at[at, step], got_b.at[at, step])

    others = (1, 3, 2)

    def higher(action):
        for to in range(1, RING):
            pl.when(to > y)(functools.partial(action, to))

    def lower(action):
        for at in range(RING - 2, -1, -1):
            pl.when(at < y)(functools.partial(action, at))

    for step in others:
        a_over_z(step).start()
    higher(lambda to: b_over_y(to).start())
    for step in others:
        b_over_x(y, step).start()

    row_max[...] = jnp.full(row_max.shape, -1e30, F32)
    row_sum[...] = jnp.zeros(row_sum.shape, F32)
    accum[...] = jnp.zeros(accum.shape, F32)
    block = GROUP * rows

    def spread_a(step):
        higher(lambda to: a_over_y(to, step).start())
        give_a(y, step).start()

    def spread_b(at):
        for step in others:
            b_from_x(at, step).wait_recv()
        for step in others:
            b_over_z(at, step).start()
        give_b(at, 0).start()

    loads[12].wait()
    queries = mm(normed, qw[...]).astype(BF16)
    for step in others:
        a_from_z(step).wait_recv()
    for step in others:
        a_over_x(step).start()
    spread_a(0)
    spread_b(y)

    def pass_b(at):
        b_from_y(at).wait_recv()
        for step in others:
            b_over_x(at, step).start()

    loads[13].wait()
    for h in range(heads):
        cols = slice(h * W, (h + 1) * W)
        qp_ref[h] = (mm_nt(queries[:, cols], ku[:, cols]) * SCORE_SCALE).astype(BF16)
    lower(pass_b)
    for step in others:
        a_from_x(step).wait_recv()
        spread_a(step)
    lower(spread_b)

    def work(at, pair, part, masked):
        steps = (pair * 2, pair * 2 + 1)
        if part == 0:
            places = [(turn(x, s), 0) for s in steps]
            keys = [
                lat_a[c, at, turn(x, s)].reshape(line, latent) for s in steps for c in range(2)
            ]
        else:
            keys = [
                lat_b[c, at, turn(z, s)].reshape(line, latent) for s in steps for c in range(2)
            ]
        count = len(keys) * line

        def positions(shape):
            column = iota(shape, 1)
            slot, inner = (column // PART) % RING, column % PART
            half = (column // line) % 2
            inner = inner + half * (2 * PART) + part * PART
            first_step = column < 2 * line
            if part == 0:
                block_x = jnp.where(first_step, turn(x, steps[0]), turn(x, steps[1]))
                chip = block_x * RING + slot
            else:
                block_z = jnp.where(first_step, turn(z, steps[0]), turn(z, steps[1]))
                chip = slot * RING + block_z
            return (at * RING * RING + chip) * rows + inner

        keys = jnp.concatenate(keys, axis=0)
        for b in range(0, heads, GROUP):
            place = slice(b * rows, b * rows + block)
            queries = qp_ref[b : b + GROUP].reshape(block, latent)
            scores = mm_nt(queries, keys)
            if masked:
                query_pos = here * rows + iota((block, count), 0) % rows
                scores = jnp.where(positions((block, count)) <= query_pos, scores, -2e30)
            old = row_max[place, :]
            new = jnp.maximum(old, jnp.max(scores, axis=-1, keepdims=True))
            row_max[place, :] = new
            shrink = jnp.exp2(old - new)
            probs = [jnp.exp2(scores[:, c : c + W] - new) for c in range(0, count, W)]
            added = row_sum[place, :] * shrink
            for p in probs:
                added = added + p
            row_sum[place, :] = added
            mixed = mm(jnp.concatenate([p.astype(BF16) for p in probs], axis=1), keys)
            accum[place, :] = accum[place, :] * jnp.concatenate([shrink] * (latent // W), axis=1) + mixed

    def fetch_a(at, pair):
        for s in range(2):
            step = pair * 2 + s
            a_from_y(at, step).wait_recv()
            give_a(at, step).start()

    def fetch_b(at, pair):
        for s in range(2):
            step = pair * 2 + s

            def far():
                b_from_z(at, step).wait_recv()
                give_b(at, step).start()

            pl.when(step > 0)(far)

    def ready_a(at, pair):
        for s in range(2):
            take_a(at, pair * 2 + s).wait_recv()

    def ready_b(at, pair):
        for s in range(2):
            take_b(at, pair * 2 + s).wait_recv()

    def loop(begin, end, visit):
        lax.fori_loop(begin, end, lambda i, nothing: (visit(i), nothing)[1], 0)

    fetch_b(y, 0)

    def own(pair):
        ready_a(y, pair)
        work(y, pair, 0, True)

        def next_a():
            fetch_a(y - 1, 0)

        pl.when(jnp.logical_and(pair == 1, y > 0))(next_a)
        pl.when(pair == 0)(lambda: fetch_b(y, 1))
        ready_b(y, pair)
        work(y, pair, 1, True)

    loop(0, 2, own)

    def earlier(i):
        at, pair = y - 1 - i // 2, i % 2
        fetch_b(at, pair)
        ready_a(at, pair)
        work(at, pair, 0, False)
        following = y - 1 - (i + 1) // 2

        @pl.when(following >= 0)
        def _():
            fetch_a(following, (i + 1) % 2)

        ready_b(at, pair)
        work(at, pair, 1, False)

    loop(0, 2 * y, earlier)

    loads[14].wait()
    for h in range(heads):
        place = slice(h * rows, (h + 1) * rows)
        row_total = jnp.sum(row_sum[place, :], axis=-1, keepdims=True)
        mixed = accum[place, :] / row_total
        high, low = halves(mixed)
        cols = slice(h * W, (h + 1) * W)
        up = vu_ref[:, cols]
        out_ref[:, cols] = (mm(high, up) + mm(low, up)).astype(BF16)

    for step in others:
        a_over_z(step).wait_send()
        a_over_x(step).wait_send()

    def drain_up(to):
        b_over_y(to).wait_send()
        for step in range(RING):
            a_over_y(to, step).wait_send()

    higher(drain_up)

    def drain(at):
        for step in range(1, RING):
            b_over_x(at, step).wait_send()
            b_over_z(at, step).wait_send()
        for step in range(RING):
            give_a(at, step).wait_send()
            give_b(at, step).wait_send()

    loop(0, y + 1, drain)


    for step in range(1, heads):
        map_to(member(step)[0]).wait_send()
        send_state(step).wait_send()
    for step in range(1, groups):
        peer, copy = send_total(step)
        pl.when(peer > mine)(copy.wait_send)
    for p in range(PIECES):
        swap(p).wait_send()


def layer(q, k, v, ld, beta, gate, residual, out_gain, hidden_gain, latent_gain, ow, lw, qw, ku, vu):
    heads = beta.shape[0]
    rows, width = residual.shape
    latent = lw.shape[1]
    groups = lax.axis_size("seq") // heads
    vm = pl.BlockSpec(memory_space=pltpu.VMEM)
    anywhere = pl.BlockSpec(memory_space=pl.ANY)
    dma = pltpu.SemaphoreType.DMA
    operands = (q, k, v, ld, beta, gate, residual, out_gain, hidden_gain, latent_gain, ow, lw, qw, ku, vu)
    message = (W + 16, 2 * W)
    one, two = dma((RING,)), dma((RING, RING))
    return pl.pallas_call(
        layer_kernel,
        out_shape=(
            jax.ShapeDtypeStruct((rows, width), BF16),
            jax.ShapeDtypeStruct((rows, heads * W), BF16),
        ),
        in_specs=[anywhere] * len(operands),
        out_specs=(vm, vm),
        scratch_shapes=[pltpu.VMEM(a.shape, a.dtype) for a in operands] + [
            pltpu.VMEM((heads,) + message, BF16),
            pltpu.VMEM((rows, heads * W), F32),
            pltpu.VMEM((rows, heads * W), BF16),
            pltpu.VMEM((heads,) + message, BF16),
            pltpu.VMEM(message, BF16),
            pltpu.VMEM((groups,) + message, BF16),
            pltpu.VMEM((heads, W, W), BF16),
            pltpu.VMEM((heads, W, W), BF16),
            pltpu.VMEM((PIECES, rows, width // PIECES), F32),
            pltpu.VMEM((PIECES, rows, width // PIECES), F32),
            pltpu.VMEM((heads, rows, latent), BF16),
            pltpu.VMEM((2, RING, RING, RING, PART, latent), BF16),
            pltpu.VMEM((2, RING, RING, RING, PART, latent), BF16),
            pltpu.VMEM((heads * rows, W), F32),
            pltpu.VMEM((heads * rows, W), F32),
            pltpu.VMEM((heads * rows, latent), F32),
            dma((len(operands),)),
            dma((heads,)), dma((heads,)), dma((groups,)), dma((groups,)),
            dma((heads,)), dma((heads,)), dma((PIECES,)), dma((PIECES,)),
            one, one, one, one, two, two, one, one, two, two, two, two, two, two, two, two,
        ],
        compiler_params=pltpu.CompilerParams(
            collective_id=0, has_side_effects=True, vmem_limit_bytes=60 * 2**20
        ),
        name="layer",
    )(*operands)


def body(
    residual, kda_query, kda_key, kda_value, log_decay, beta_logit, out_gate, out_gain, out_weight,
    hidden_gain, query_weight, latent_weight, latent_gain, key_up_weight, value_up_weight,
):
    return layer(
        kda_query, kda_key, kda_value, log_decay, beta_logit.T, out_gate, residual, out_gain[None],
        hidden_gain.reshape(-1, W), latent_gain[None], out_weight, latent_weight, query_weight, key_up_weight,
        value_up_weight,
    )


def solution(mesh):
    in_specs = (
        P("seq", None),
        P("seq", "head"),
        P("seq", "head"),
        P("seq", "head"),
        P("seq", "head"),
        P("seq", "head"),
        P("seq", "head"),
        P(),
        P("head", None),
        P(),
        P(None, "head"),
        P(),
        P(),
        P(None, "head"),
        P(None, "head"),
    )
    out_specs = (P("seq", None), P("seq", "head"))
    return jax.shard_map(body, mesh=mesh, in_specs=in_specs, out_specs=out_specs, check_vma=False)
```

time: 178 us -> 91.1 us (0.51)
  the two profiles are of different devices: /device:TPU:31 before, /device:TPU:24 now
where the time goes in v3:
time: 91.1 us; the launch traced here: 90.6 us
  Pallas kernels  86.4 us (95%)
  local copies, waits for them, and re-layouts  3.59 us (4%)
    pallas_call x1, Pallas kernels, layer(): pl.pallas_call(layer_kernel, out_shape=(jax.ShapeDtypeStruct((rows, width...  86.4 us
    unnamed x2, local copies, waits for them, and re-layouts  3.59 us

profile of v3, /device:TPU:24, one launch (start us, length us, event | category | flops | bytes accessed | tf_op | source)
XLA Modules:
  0.0 90.6 jit_solution(18300711537771679669)
XLA Ops:
  0.6 86.4 %layer.1 = (bf16[128,2304]{1,0:T(8,128)(2,1)}, bf16[128,1024]{1,0:T(8,128)(2,1)}) custom-call(bf16[128,1024]{1,0:T(8,128)(2,1)} %q_hbm.1, bf16[128,1024]{1,0:T(8,128)(2,1)} %k_hbm.1, bf16[128,1024]{1,0:T(8,128)(2,1)} %v_hbm.1, f32[128,1024]{1,0:T(8,128)} %ld_hbm.1, f32[8,128]{1,0:T(8,128)} %bitcast.5, bf16[128,1024]{1,0:T(8,128)(2,1)} %gate_hbm.1, ...), custom_call_target="tpu_custom_call" | custom-call | tf_op jit(solution)/shard_map/layer/pallas_call | solution.py:643
  87.0 1.9 %copy.19 = bf16[128,2304]{1,0:T(8,128)(2,1)} copy(bf16[128,2304]{1,0:T(8,128)(2,1)} %get-tuple-element.4) | data formatting | bytes 1179648
  88.9 1.7 %copy.20 = bf16[128,1024]{1,0:T(8,128)(2,1)} copy(bf16[128,1024]{1,0:T(8,128)(2,1)} %get-tuple-element.5) | data formatting | bytes 524288

commit v4 on v3

--- a/solution.py
+++ b/solution.py
@@ -56,7 +56,7 @@
 SCORE_SCALE = W ** (-0.5) * 1.4426950408889634
 RING = 4
 PART = 32
-GROUP = 4
+GROUP = 8
 
 
 def pack_diag(closing):
@@ -153,9 +153,9 @@
     hidden_o, out_ref,
     q_in, k_in, v_in, ld_in, beta_in, gate, residual, out_gain, hidden_gain, latent_gain, ow, lw, qw, ku, vu_ref,
     msg, base, carry, got, total, totals, states, state_in, partial, other,
-    qp_ref, lat_a, lat_b, row_max, row_sum, accum,
+    qp_ref, lat_a, lat_b, row_max, row_sum, accum, mail_out, mail_in, note_out, note_in,
     load_sem, send_a, recv_a, send_b, recv_b, send_c, recv_c, send_p, recv_p,
-    sa1, ra1, sa2, ra2, sa3, ra3, sb1, rb1, sb2, rb2, sb3, rb3, swap_a, got_a, swap_b, got_b,
+    sa1, ra1, sa2, ra2, sa3, ra3, sb1, rb1, sb2, rb2, sb3, rb3, swap_a, got_a, swap_b, got_b, sm, rm,
 ):
     heads = msg.shape[0]
     groups = totals.shape[0]
@@ -358,13 +358,6 @@
     raw = raw * lax.rsqrt(jnp.mean(raw * raw, axis=-1, keepdims=True) + EPS)
     raw = (raw * latent_gain[...]).astype(BF16)
 
-    def place_parts(which):
-        first = which * 2 * PART
-        lat_a[core, y, x, z] = raw[first : first + PART]
-        lat_b[core, y, z, x] = raw[first + PART : first + 2 * PART]
-
-    for which in range(2):
-        pl.when(core == which)(functools.partial(place_parts, which))
     def remote(place, peer, send, recv):
         return pltpu.make_async_remote_copy(
             src_ref=place, dst_ref=place, send_sem=send, recv_sem=recv,
@@ -391,27 +384,39 @@
     def a_from_y(at, step):
         return remote(lat_a.at[core, at, turn(x, step)], sibling, sa3.at[at, 0], ra3.at[at, step])
 
+    def axes(at):
+        return jnp.where(at < RING // 2, x, z), jnp.where(at < RING // 2, z, x)
+
+    def along(at, first, second):
+        return device(y, jnp.where(at < RING // 2, first, second), jnp.where(at < RING // 2, second, first))
+
     def b_over_y(to):
-        return remote(lat_b.at[core, y, z, x], device(to, x, z), sb1.at[to], rb1.at[y])
+        u, v = axes(y)
+        return remote(lat_b.at[core, y, u, v], device(to, x, z), sb1.at[to], rb1.at[y])
 
     def b_from_y(at):
-        return remote(lat_b.at[core, at, z, x], sibling, sb1.at[at], rb1.at[at])
-
-    def b_over_x(at, step):
+        u, v = axes(at)
+        return remote(lat_b.at[core, at, u, v], sibling, sb1.at[at], rb1.at[at])
+
+    def b_over_v(at, step):
+        u, v = axes(at)
         return remote(
-            lat_b.at[core, at, z, x], device(y, turn(x, step), z), sb2.at[at, step], rb2.at[at, RING - step]
-        )
-
-    def b_from_x(at, step):
-        return remote(lat_b.at[core, at, z, turn(x, step)], sibling, sb2.at[at, 0], rb2.at[at, step])
-
-    def b_over_z(at, step):
+            lat_b.at[core, at, u, v], along(at, u, turn(v, step)), sb2.at[at, step], rb2.at[at, RING - step]
+        )
+
+    def b_from_v(at, step):
+        u, v = axes(at)
+        return remote(lat_b.at[core, at, u, turn(v, step)], sibling, sb2.at[at, 0], rb2.at[at, step])
+
+    def b_over_u(at, step):
+        u, v = axes(at)
         return remote(
-            lat_b.at[core, at, z], device(y, x, turn(z, step)), sb3.at[at, step], rb3.at[at, RING - step]
-        )
-
-    def b_from_z(at, step):
-        return remote(lat_b.at[core, at, turn(z, step)], sibling, sb3.at[at, 0], rb3.at[at, step])
+            lat_b.at[core, at, u], along(at, turn(u, step), v), sb3.at[at, step], rb3.at[at, RING - step]
+        )
+
+    def b_from_u(at, step):
+        u, v = axes(at)
+        return remote(lat_b.at[core, at, turn(u, step)], sibling, sb3.at[at, 0], rb3.at[at, step])
 
     def give_a(at, step):
         return remote(lat_a.at[core, at, turn(x, step)], sibling, swap_a.at[at, step], got_a.at[at, step])
@@ -420,30 +425,55 @@
         return remote(lat_a.at[1 - core, at, turn(x, step)], sibling, swap_a.at[at, step], got_a.at[at, step])
 
     def give_b(at, step):
-        return remote(lat_b.at[core, at, turn(z, step)], sibling, swap_b.at[at, step], got_b.at[at, step])
+        return remote(lat_b.at[core, at, turn(axes(at)[0], step)], sibling, swap_b.at[at, step], got_b.at[at, step])
 
     def take_b(at, step):
-        return remote(lat_b.at[1 - core, at, turn(z, step)], sibling, swap_b.at[at, step], got_b.at[at, step])
+        return remote(lat_b.at[1 - core, at, turn(axes(at)[0], step)], sibling, swap_b.at[at, step], got_b.at[at, step])
 
     others = (1, 3, 2)
 
+    partner = device(RING - 1 - y, x, z)
+
+    def mail():
+        return pltpu.make_async_remote_copy(
+            src_ref=mail_out, dst_ref=mail_in, send_sem=sm.at[0], recv_sem=rm.at[0],
+            device_id=partner, device_id_type=MESH,
+        )
+
+    def note():
+        return pltpu.make_async_remote_copy(
+            src_ref=note_out, dst_ref=note_in, send_sem=sm.at[1], recv_sem=rm.at[1],
+            device_id=partner, device_id_type=MESH,
+        )
+
     def higher(action):
-        for to in range(1, RING):
-            pl.when(to > y)(functools.partial(action, to))
+        for to in range(RING - 1, 0, -1):
+            pl.when(jnp.logical_and(to > y, to - y < RING - 1))(functools.partial(action, to))
 
     def lower(action):
         for at in range(RING - 2, -1, -1):
-            pl.when(at < y)(functools.partial(action, at))
-
+            pl.when(jnp.logical_and(at < y, y - at < RING - 1))(functools.partial(action, at))
+
+    def place_parts(which):
+        first = which * 2 * PART
+        lat_a[core, y, x, z] = raw[first : first + PART]
+        u, v = axes(y)
+        lat_b[core, y, u, v] = raw[first + PART : first + 2 * PART]
+
+    for which in range(2):
+        pl.when(core == which)(functools.partial(place_parts, which))
     for step in others:
         a_over_z(step).start()
     higher(lambda to: b_over_y(to).start())
     for step in others:
-        b_over_x(y, step).start()
-
-    row_max[...] = jnp.full(row_max.shape, -1e30, F32)
-    row_sum[...] = jnp.zeros(row_sum.shape, F32)
-    accum[...] = jnp.zeros(accum.shape, F32)
+        b_over_v(y, step).start()
+
+    def clear():
+        row_max[...] = jnp.full(row_max.shape, -1e30, F32)
+        row_sum[...] = jnp.zeros(row_sum.shape, F32)
+        accum[...] = jnp.zeros(accum.shape, F32)
+
+    clear()
     block = GROUP * rows
 
     def spread_a(step):
@@ -452,13 +482,14 @@
 
     def spread_b(at):
         for step in others:
-            b_from_x(at, step).wait_recv()
+            b_from_v(at, step).wait_recv()
         for step in others:
-            b_over_z(at, step).start()
+            b_over_u(at, step).start()
         give_b(at, 0).start()
 
     loads[12].wait()
-    queries = mm(normed, qw[...]).astype(BF16)
+    mail_out[...] = mm(normed, qw[...]).astype(BF16)
+    pl.when(y == RING - 1)(lambda: mail().start())
     for step in others:
         a_from_z(step).wait_recv()
     for step in others:
@@ -469,53 +500,28 @@
     def pass_b(at):
         b_from_y(at).wait_recv()
         for step in others:
-            b_over_x(at, step).start()
-
+            b_over_v(at, step).start()
+
+    lower(pass_b)
     loads[13].wait()
-    for h in range(heads):
-        cols = slice(h * W, (h + 1) * W)
-        qp_ref[h] = (mm_nt(queries[:, cols], ku[:, cols]) * SCORE_SCALE).astype(BF16)
-    lower(pass_b)
-    for step in others:
-        a_from_x(step).wait_recv()
-        spread_a(step)
-    lower(spread_b)
-
-    def work(at, pair, part, masked):
-        steps = (pair * 2, pair * 2 + 1)
-        if part == 0:
-            places = [(turn(x, s), 0) for s in steps]
-            keys = [
-                lat_a[c, at, turn(x, s)].reshape(line, latent) for s in steps for c in range(2)
-            ]
-        else:
-            keys = [
-                lat_b[c, at, turn(z, s)].reshape(line, latent) for s in steps for c in range(2)
-            ]
-        count = len(keys) * line
-
-        def positions(shape):
-            column = iota(shape, 1)
-            slot, inner = (column // PART) % RING, column % PART
-            half = (column // line) % 2
-            inner = inner + half * (2 * PART) + part * PART
-            first_step = column < 2 * line
-            if part == 0:
-                block_x = jnp.where(first_step, turn(x, steps[0]), turn(x, steps[1]))
-                chip = block_x * RING + slot
-            else:
-                block_z = jnp.where(first_step, turn(z, steps[0]), turn(z, steps[1]))
-                chip = slot * RING + block_z
-            return (at * RING * RING + chip) * rows + inner
-
-        keys = jnp.concatenate(keys, axis=0)
+
+    def absorb(queries):
+        for h in range(heads):
+            cols = slice(h * W, (h + 1) * W)
+            qp_ref[h] = (mm_nt(queries[:, cols], ku[:, cols]) * SCORE_SCALE).astype(BF16)
+
+    absorb(mail_out)
+
+    def attend(pieces, mask):
+        keys = jnp.concatenate([piece.reshape(line, latent) for piece in pieces], axis=0)
+        count = keys.shape[0]
         for b in range(0, heads, GROUP):
             place = slice(b * rows, b * rows + block)
             queries = qp_ref[b : b + GROUP].reshape(block, latent)
             scores = mm_nt(queries, keys)
-            if masked:
+            if mask is not None:
                 query_pos = here * rows + iota((block, count), 0) % rows
-                scores = jnp.where(positions((block, count)) <= query_pos, scores, -2e30)
+                scores = jnp.where(mask((1, count)) <= query_pos, scores, -2e30)
             old = row_max[place, :]
             new = jnp.maximum(old, jnp.max(scores, axis=-1, keepdims=True))
             row_max[place, :] = new
@@ -528,74 +534,125 @@
             mixed = mm(jnp.concatenate([p.astype(BF16) for p in probs], axis=1), keys)
             accum[place, :] = accum[place, :] * jnp.concatenate([shrink] * (latent // W), axis=1) + mixed
 
-    def fetch_a(at, pair):
+    def own_lines(step):
+        u = turn(axes(y)[0], step)
+        line_x = turn(x, step)
+        return lat_a[0, y, line_x], lat_a[1, y, line_x], lat_b[0, y, u], lat_b[1, y, u]
+
+    def own(step):
+        u = turn(axes(y)[0], step)
+        line_x = turn(x, step)
+
+        def positions(shape):
+            column = iota(shape, 1)
+            slot, inner, piece = (column // PART) % RING, column % PART, column // line
+            part_b = piece // 2
+            chip_a = line_x * RING + slot
+            chip_b = jnp.where(y < RING // 2, u * RING + slot, slot * RING + u)
+            chip = jnp.where(part_b == 1, chip_b, chip_a)
+            return (y * RING * RING + chip) * rows + (piece % 2) * (2 * PART) + part_b * PART + inner
+
+        take_a(y, step).wait_recv()
+        take_b(y, step).wait_recv()
+        attend(own_lines(step), positions)
+
+    def fetch_a(at, step):
+        a_from_y(at, step).wait_recv()
+        give_a(at, step).start()
+
+    def fetch_b(at, step):
+        def far():
+            b_from_u(at, step).wait_recv()
+            give_b(at, step).start()
+
+        pl.when(step > 0)(far)
+
+    def both(pair, visit):
         for s in range(2):
-            step = pair * 2 + s
-            a_from_y(at, step).wait_recv()
-            give_a(at, step).start()
-
-    def fetch_b(at, pair):
-        for s in range(2):
-            step = pair * 2 + s
-
-            def far():
-                b_from_z(at, step).wait_recv()
-                give_b(at, step).start()
-
-            pl.when(step > 0)(far)
-
-    def ready_a(at, pair):
-        for s in range(2):
-            take_a(at, pair * 2 + s).wait_recv()
-
-    def ready_b(at, pair):
-        for s in range(2):
-            take_b(at, pair * 2 + s).wait_recv()
+            visit(jnp.where(pair == 0, s, RING - 1 - s))
 
     def loop(begin, end, visit):
         lax.fori_loop(begin, end, lambda i, nothing: (visit(i), nothing)[1], 0)
 
-    fetch_b(y, 0)
-
-    def own(pair):
-        ready_a(y, pair)
-        work(y, pair, 0, True)
-
-        def next_a():
-            fetch_a(y - 1, 0)
-
-        pl.when(jnp.logical_and(pair == 1, y > 0))(next_a)
-        pl.when(pair == 0)(lambda: fetch_b(y, 1))
-        ready_b(y, pair)
-        work(y, pair, 1, True)
-
-    loop(0, 2, own)
+    lower(spread_b)
+    own(0)
+    for step in others:
+        a_from_x(step).wait_recv()
+        spread_a(step)
+    for step in others:
+        fetch_b(y, step)
+
+    def own_round(i):
+        own(jnp.where(i == 0, 1, jnp.where(i == 1, 3, 2)))
+
+    loop(0, RING - 1, own_round)
+
+    last_plane = jnp.where(y == RING - 1, 1, 0)
+    pl.when(y > 0)(lambda: both(0, lambda step: fetch_a(y - 1, step)))
 
     def earlier(i):
         at, pair = y - 1 - i // 2, i % 2
-        fetch_b(at, pair)
-        ready_a(at, pair)
-        work(at, pair, 0, False)
+        steps = (jnp.where(pair == 0, 0, 3), jnp.where(pair == 0, 1, 2))
+        both(pair, lambda step: fetch_b(at, step))
+        both(pair, lambda step: take_a(at, step).wait_recv())
+        attend([lat_a[c, at, turn(x, step)] for step in steps for c in range(2)], None)
         following = y - 1 - (i + 1) // 2
 
-        @pl.when(following >= 0)
+        @pl.when(following >= last_plane)
         def _():
-            fetch_a(following, (i + 1) % 2)
-
-        ready_b(at, pair)
-        work(at, pair, 1, False)
-
-    loop(0, 2 * y, earlier)
+            both((i + 1) % 2, lambda step: fetch_a(following, step))
+
+        both(pair, lambda step: take_b(at, step).wait_recv())
+        u = axes(at)[0]
+        attend([lat_b[c, at, turn(u, step)] for step in steps for c in range(2)], None)
+
+    loop(0, 2 * (y - last_plane), earlier)
 
     loads[14].wait()
-    for h in range(heads):
+
+    def result(h):
         place = slice(h * rows, (h + 1) * rows)
         row_total = jnp.sum(row_sum[place, :], axis=-1, keepdims=True)
-        mixed = accum[place, :] / row_total
-        high, low = halves(mixed)
-        cols = slice(h * W, (h + 1) * W)
-        up = vu_ref[:, cols]
-        out_ref[:, cols] = (mm(high, up) + mm(low, up)).astype(BF16)
+        high, low = halves(accum[place, :] / row_total)
+        up = vu_ref[:, h * W : (h + 1) * W]
+        return mm(high, up) + mm(low, up), row_max[place, :] + jnp.log2(row_total)
+
+    @pl.when(y < RING - 1)
+    def _():
+        for h in range(heads):
+            out_ref[:, h * W : (h + 1) * W] = result(h)[0].astype(BF16)
+
+    @pl.when(y == 0)
+    def _():
+        mail().wait_recv()
+        absorb(mail_in)
+        clear()
+        loop(0, RING, lambda step: attend(own_lines(step), None))
+        lane = iota((rows, W), 1)
+        level = jnp.zeros((rows, W), F32)
+        for h in range(heads):
+            mixed, log_sum = result(h)
+            mail_out[:, h * W : (h + 1) * W] = mixed.astype(BF16)
+            level = jnp.where(lane == h, log_sum, level)
+        note_out[...] = level
+        note().start()
+        mail().start()
+        note().wait_send()
+        mail().wait_send()
+
+    @pl.when(y == RING - 1)
+    def _():
+        mail().wait_send()
+        note().wait_recv()
+        mail().wait_recv()
+        for h in range(heads):
+            cols = slice(h * W, (h + 1) * W)
+            mixed, log_sum = result(h)
+            gap = log_sum - note_in[:, h : h + 1]
+            far = mail_in[:, cols].astype(F32)
+            out_ref[:, cols] = (
+                mixed / (1.0 + jnp.exp2(-gap)) + far / (1.0 + jnp.exp2(gap))
+            ).astype(BF16)
 
     for step in others:
         a_over_z(step).wait_send()
@@ -610,13 +667,13 @@
 
     def drain(at):
         for step in range(1, RING):
-            b_over_x(at, step).wait_send()
-            b_over_z(at, step).wait_send()
+            b_over_v(at, step).wait_send()
+            b_over_u(at, step).wait_send()
         for step in range(RING):
             give_a(at, step).wait_send()
             give_b(at, step).wait_send()
 
-    loop(0, y + 1, drain)
+    loop(last_plane, y + 1, drain)
 
 
     for step in range(1, heads):
@@ -665,10 +722,15 @@
             pltpu.VMEM((heads * rows, W), F32),
             pltpu.VMEM((heads * rows, W), F32),
             pltpu.VMEM((heads * rows, latent), F32),
+            pltpu.VMEM((rows, heads * W), BF16),
+            pltpu.VMEM((rows, heads * W), BF16),
+            pltpu.VMEM((rows, W), F32),
+            pltpu.VMEM((rows, W), F32),
             dma((len(operands),)),
             dma((heads,)), dma((heads,)), dma((groups,)), dma((groups,)),
             dma((heads,)), dma((heads,)), dma((PIECES,)), dma((PIECES,)),
             one, one, one, one, two, two, one, one, two, two, two, two, two, two, two, two,
+            dma((2,)), dma((2,)),
         ],
         compiler_params=pltpu.CompilerParams(
             collective_id=0, has_side_effects=True, vmem_limit_bytes=60 * 2**20
@@ -677,15 +739,32 @@
     )(*operands)
 
 
+def finish_kernel(hidden_in, attended_in, hidden_out, attended_out):
+    hidden_out[...] = hidden_in[...]
+    attended_out[...] = attended_in[...]
+
+
+def finish(hidden, attended):
+    vm = pl.BlockSpec(memory_space=pltpu.VMEM)
+    return pl.pallas_call(
+        finish_kernel,
+        out_shape=tuple(jax.ShapeDtypeStruct(a.shape, a.dtype) for a in (hidden, attended)),
+        in_specs=[vm] * 2,
+        out_specs=(vm, vm),
+        name="finish",
+    )(hidden, attended)
+
+
 def body(
     residual, kda_query, kda_key, kda_value, log_decay, beta_logit, out_gate, out_gain, out_weight,
     hidden_gain, query_weight, latent_weight, latent_gain, key_up_weight, value_up_weight,
 ):
-    return layer(
+    hidden, attended = layer(
         kda_query, kda_key, kda_value, log_decay, beta_logit.T, out_gate, residual, out_gain[None],
         hidden_gain.reshape(-1, W), latent_gain[None], out_weight, latent_weight, query_weight, key_up_weight,
         value_up_weight,
     )
+    return finish(hidden, attended)
 
 
 def solution(mesh):

time: 91.1 us -> 83.7 us (0.919)
  Pallas kernels: 86.4 us -> 82.6 us
  local copies, waits for them, and re-layouts: 3.59 us -> 0 us
    pallas_call x1, Pallas kernels: 86.4 us -> 80.6 us  [layer(): pl.pallas_call(layer_kernel, out_shape=(jax.ShapeDtypeStruct((rows, width...]
    unnamed x2 -> x0, local copies, waits for them, and re-layouts: 3.59 us -> none
    pallas_call x0 -> x1, Pallas kernels: none -> 2.06 us  [finish(): pl.pallas_call(finish_kernel, out_shape=tuple((jax.ShapeDtypeStruct(a.sha...]
where the time goes in v4:
time: 83.7 us; the launch traced here: 83.3 us
  Pallas kernels  82.6 us (99%)
    pallas_call x1, Pallas kernels, layer(): pl.pallas_call(layer_kernel, out_shape=(jax.ShapeDtypeStruct((rows, width...  80.6 us
    pallas_call x1, Pallas kernels, finish(): pl.pallas_call(finish_kernel, out_shape=tuple((jax.ShapeDtypeStruct(a.sha...  2.06 us

profile of v4, /device:TPU:24, one launch (start us, length us, event | category | flops | bytes accessed | tf_op | source)
XLA Modules:
  0.0 83.3 jit_solution(4475453372604096460)
XLA Ops:
  0.6 80.6 %layer.1 = (bf16[128,2304]{1,0:T(8,128)(2,1)}, bf16[128,1024]{1,0:T(8,128)(2,1)}) custom-call(bf16[128,1024]{1,0:T(8,128)(2,1)} %q_hbm.1, bf16[128,1024]{1,0:T(8,128)(2,1)} %k_hbm.1, bf16[128,1024]{1,0:T(8,128)(2,1)} %v_hbm.1, f32[128,1024]{1,0:T(8,128)} %ld_hbm.1, f32[8,128]{1,0:T(8,128)} %bitcast.5, bf16[128,1024]{1,0:T(8,128)(2,1)} %gate_hbm.1, ...), custom_call_target="tpu_custom_call" | custom-call | tf_op jit(solution)/shard_map/layer/pallas_call | solution.py:700
  81.2 2.1 %finish.1 = (bf16[128,2304]{1,0:T(8,128)(2,1)}, bf16[128,1024]{1,0:T(8,128)(2,1)}) custom-call(bf16[128,2304]{1,0:T(8,128)(2,1)} %get-tuple-element.4.hidden_in, bf16[128,1024]{1,0:T(8,128)(2,1)} %get-tuple-element.5.attended_in), custom_call_target="tpu_custom_call" | custom-call | tf_op jit(solution)/shard_map/finish/pallas_call | solution.py:749

commit v5 on v4

--- a/solution.py
+++ b/solution.py
@@ -57,6 +57,7 @@
 RING = 4
 PART = 32
 GROUP = 8
+DELTA_GROUP = 8
 
 
 def pack_diag(closing):
@@ -81,70 +82,83 @@
     return out + later[:, W:]
 
 
-def delta_part(q_ref, k_ref, v_ref, ld_ref, beta_ref, msg_ref, base_ref, carry_ref, sent):
-    rows = q_ref.shape[0]
-    heads = q_ref.shape[1] // W
+def unit(values):
+    return values * lax.rsqrt(jnp.sum(values * values, axis=-1, keepdims=True) + EPS)
+
+
+def triangle(rows):
     ti, si = iota((rows, rows), 0), iota((rows, rows), 1)
+    return ti, si, si < ti
+
+
+def invert(lowers):
+    rows = lowers[0].shape[0]
+    ti, si, strict = triangle(rows)
+    eye = jnp.where(si == ti, 1.0, 0.0)
+    level = jnp.logical_and((ti // 2) == (si // 2), strict)
+    found = [eye - jnp.where(level, low, 0.0) for low in lowers]
+    size = 2
+    while size < rows:
+        level = jnp.logical_and((ti // (2 * size)) == (si // (2 * size)), (ti // size) > (si // size))
+        inner = [mm4(jnp.where(level, low, 0.0), x) for low, x in zip(lowers, found)]
+        found = [x - mm4(x, y) for x, y in zip(found, inner)]
+        size *= 2
+    return found
+
+
+def delta_maps(k_ref, v_ref, ld_ref, beta_ref, msg_ref, cum_ref, solved_ref, sent):
+    rows = k_ref.shape[0]
+    heads = k_ref.shape[1] // W
+    ti, si, strict = triangle(rows)
     ones = jnp.where(si <= ti, 1.0, 0.0).astype(BF16)
-    strict = si < ti
-    through = si <= ti
-    eye = jnp.where(si == ti, 1.0, 0.0)
     rates = (1.0 / (1.0 + jnp.exp(-beta_ref[...]))).T
 
-    def stage_one(h):
+    def prepare(h):
         cols = slice(h * W, (h + 1) * W)
         ld = ld_ref[:, cols]
         high, rest = halves(ld)
         low = (ld - high.astype(F32) - rest.astype(F32)).astype(BF16)
         cum = mm(ones, high) + (mm(ones, rest) + mm(ones, low))
+        cum_ref[:, cols] = cum
         mid = cum[rows // 2 - 1 : rows // 2, :]
         end = cum[rows - 1 : rows, :]
-        key = k_ref[:, cols].astype(F32)
-        key = key * lax.rsqrt(jnp.sum(key * key, axis=-1, keepdims=True) + EPS)
-        query = q_ref[:, cols].astype(F32)
-        query = query * lax.rsqrt(jnp.sum(query * query, axis=-1, keepdims=True) + EPS)
-        forward = jnp.exp(cum - mid)
-        mixed = mm4_nt(
-            jnp.concatenate([key * forward, query * forward], axis=0), key * jnp.exp(mid - cum)
-        )
+        key = unit(k_ref[:, cols].astype(F32))
+        mixed = mm4_nt(key * jnp.exp(cum - mid), key * jnp.exp(mid - cum))
         rate = rates[:, h : h + 1]
-        lower = jnp.where(strict, mixed[:rows], 0.0) * rate
-        mix = jnp.where(through, mixed[rows:], 0.0)
-        growth = jnp.exp(cum)
+        lower = jnp.where(strict, mixed, 0.0) * rate
         right = jnp.concatenate(
-            [rate * v_ref[:, cols].astype(F32), rate * (key * growth)], axis=1
-        )
-        tail = (key * jnp.exp(end - cum)).T
-        return lower, mix, right, tail, query * growth, jnp.exp(end)
-
-    def invert(lowers):
-        level = jnp.logical_and((ti // 2) == (si // 2), strict)
-        found = [eye - jnp.where(level, low, 0.0) for low in lowers]
-        size = 2
-        while size < rows:
-            level = jnp.logical_and((ti // (2 * size)) == (si // (2 * size)),
-                                    (ti // size) > (si // size))
-            inner = [mm4(jnp.where(level, low, 0.0), x) for low, x in zip(lowers, found)]
-            found = [x - mm4(x, y) for x, y in zip(found, inner)]
-            size *= 2
-        return found
-
-    group = 4
-    for start in range(0, heads, group):
-        made = [stage_one(h) for h in range(start, start + group)]
+            [rate * v_ref[:, cols].astype(F32), rate * (key * jnp.exp(cum))], axis=1
+        )
+        return lower, right, (key * jnp.exp(end - cum)).T, jnp.exp(end)
+
+    for start in range(0, heads, DELTA_GROUP):
+        made = [prepare(h) for h in range(start, start + DELTA_GROUP)]
         inverses = invert([m[0] for m in made])
-        for h in range(start, start + group):
-            _, mix, right, tail, query, closing = made[h - start]
-            solved = mm4(inverses[h - start], right)
+        for h, inverse, (_, right, tail, closing) in zip(
+            range(start, start + DELTA_GROUP), inverses, made
+        ):
+            solved = mm4(inverse, right)
+            solved_ref[h] = solved
             state = mm4(tail, solved)
-            out = mm4(mix, solved)
-            cols = slice(h * W, (h + 1) * W)
-            base_ref[:, cols] = out[:, :W]
-            carry_ref[:, cols] = (query - out[:, W:]).astype(BF16)
             msg_ref[h, :W, :W] = state[:, W:].astype(BF16)
             msg_ref[h, :W, W:] = state[:, :W].astype(BF16)
             msg_ref[h, W:, :] = pack_diag(closing)
-        sent(start, start + group)
+        sent(start, start + DELTA_GROUP)
+
+
+def delta_outputs(q_ref, k_ref, cum_ref, solved_ref, base_ref, carry_ref):
+    rows = k_ref.shape[0]
+    ti, si, _ = triangle(rows)
+    for h in range(k_ref.shape[1] // W):
+        cols = slice(h * W, (h + 1) * W)
+        cum = cum_ref[:, cols]
+        mid = cum[rows // 2 - 1 : rows // 2, :]
+        key = unit(k_ref[:, cols].astype(F32))
+        query = unit(q_ref[:, cols].astype(F32))
+        mixed = mm4_nt(query * jnp.exp(cum - mid), key * jnp.exp(mid - cum))
+        out = mm4(jnp.where(si <= ti, mixed, 0.0), solved_ref[h])
+        base_ref[:, cols] = out[:, :W]
+        carry_ref[:, cols] = (query * jnp.exp(cum) - out[:, W:]).astype(BF16)
 
 
 def layer_kernel(
@@ -152,8 +166,8 @@
     latent_gain_hbm, ow_hbm, lw_hbm, qw_hbm, ku_hbm, vu_hbm,
     hidden_o, out_ref,
     q_in, k_in, v_in, ld_in, beta_in, gate, residual, out_gain, hidden_gain, latent_gain, ow, lw, qw, ku, vu_ref,
-    msg, base, carry, got, total, totals, states, state_in, partial, other,
-    qp_ref, lat_a, lat_b, row_max, row_sum, accum, mail_out, mail_in, note_out, note_in,
+    cum, solved, msg, base, carry, got, total, totals, states, state_in, partial, other,
+    qp_ref, lat_a, lat_b, row_max, row_sum, accum, far_qp, far_max, far_sum, far_accum, mail_out, mail_in, note_out, note_in,
     load_sem, send_a, recv_a, send_b, recv_b, send_c, recv_c, send_p, recv_p,
     sa1, ra1, sa2, ra2, sa3, ra3, sb1, rb1, sb2, rb2, sb3, rb3, swap_a, got_a, swap_b, got_b, sm, rm,
 ):
@@ -189,15 +203,17 @@
     pl.semaphore_signal(barrier, inc=1, device_id=device(y, RING - 1 - x, z), device_id_type=MESH)
 
     pairs = (
-        (k_hbm, k_in), (ld_hbm, ld_in), (q_hbm, q_in), (v_hbm, v_in), (beta_hbm, beta_in), (gate_hbm, gate),
+        (k_hbm, k_in), (ld_hbm, ld_in), (v_hbm, v_in), (beta_hbm, beta_in), (q_hbm, q_in), (gate_hbm, gate),
         (residual_hbm, residual), (out_gain_hbm, out_gain), (hidden_gain_hbm, hidden_gain),
         (latent_gain_hbm, latent_gain), (ow_hbm, ow), (lw_hbm, lw), (qw_hbm, qw), (ku_hbm, ku), (vu_hbm, vu_ref),
     )
     loads = [pltpu.make_async_copy(src, dst, load_sem.at[i]) for i, (src, dst) in enumerate(pairs)]
-    for load in loads:
+    for load in loads[:4]:
         load.start()
-    for load in loads[:5]:
+    for load in loads[:4]:
         load.wait()
+    for load in loads[4:]:
+        load.start()
 
     def map_to(peer):
         return pltpu.make_async_remote_copy(
@@ -219,8 +235,10 @@
         for peer in range(begin, end):
             pl.when(peer != rank)(map_to(peer).start)
 
-    delta_part(q_in, k_in, v_in, ld_in, beta_in, msg, base, carry, sent)
+    delta_maps(k_in, v_in, ld_in, beta_in, msg, cum, solved, sent)
     got[rank] = msg[rank]
+    loads[4].wait()
+    delta_outputs(q_in, k_in, cum, solved, base, carry)
     for step in range(1, heads):
         map_from(member(step)[0]).wait_recv()
 
@@ -385,14 +403,20 @@
         return remote(lat_a.at[core, at, turn(x, step)], sibling, sa3.at[at, 0], ra3.at[at, step])
 
     def axes(at):
-        return jnp.where(at < RING // 2, x, z), jnp.where(at < RING // 2, z, x)
+        turned = at + RING // 2 == y
+        return jnp.where(turned, x, z), jnp.where(turned, z, x)
 
     def along(at, first, second):
-        return device(y, jnp.where(at < RING // 2, first, second), jnp.where(at < RING // 2, second, first))
+        turned = at + RING // 2 == y
+        return device(y, jnp.where(turned, first, second), jnp.where(turned, second, first))
 
     def b_over_y(to):
-        u, v = axes(y)
-        return remote(lat_b.at[core, y, u, v], device(to, x, z), sb1.at[to], rb1.at[y])
+        turned = y + RING // 2 == to
+        return pltpu.make_async_remote_copy(
+            src_ref=lat_b.at[core, y, z, x],
+            dst_ref=lat_b.at[core, y, jnp.where(turned, x, z), jnp.where(turned, z, x)],
+            send_sem=sb1.at[to], recv_sem=rb1.at[y], device_id=device(to, x, z), device_id_type=MESH,
+        )
 
     def b_from_y(at):
         u, v = axes(at)
@@ -448,11 +472,11 @@
 
     def higher(action):
         for to in range(RING - 1, 0, -1):
-            pl.when(jnp.logical_and(to > y, to - y < RING - 1))(functools.partial(action, to))
+            pl.when(jnp.logical_and(to > y, to + y != RING - 1))(functools.partial(action, to))
 
     def lower(action):
         for at in range(RING - 2, -1, -1):
-            pl.when(jnp.logical_and(at < y, y - at < RING - 1))(functools.partial(action, at))
+            pl.when(jnp.logical_and(at < y, at + y != RING - 1))(functools.partial(action, at))
 
     def place_parts(which):
         first = which * 2 * PART
@@ -468,12 +492,12 @@
     for step in others:
         b_over_v(y, step).start()
 
-    def clear():
-        row_max[...] = jnp.full(row_max.shape, -1e30, F32)
-        row_sum[...] = jnp.zeros(row_sum.shape, F32)
-        accum[...] = jnp.zeros(accum.shape, F32)
-
-    clear()
+    def clear(store):
+        store[1][...] = jnp.full(store[1].shape, -1e30, F32)
+        store[2][...] = jnp.zeros(store[2].shape, F32)
+        store[3][...] = jnp.zeros(store[3].shape, F32)
+
+    clear((qp_ref, row_max, row_sum, accum))
     block = GROUP * rows
 
     def spread_a(step):
@@ -489,7 +513,7 @@
 
     loads[12].wait()
     mail_out[...] = mm(normed, qw[...]).astype(BF16)
-    pl.when(y == RING - 1)(lambda: mail().start())
+    pl.when(y >= RING // 2)(lambda: mail().start())
     for step in others:
         a_from_z(step).wait_recv()
     for step in others:
@@ -505,42 +529,46 @@
     lower(pass_b)
     loads[13].wait()
 
-    def absorb(queries):
+    mine_store = (qp_ref, row_max, row_sum, accum)
+    far_store = (far_qp, far_max, far_sum, far_accum)
+
+    def absorb(queries, store):
         for h in range(heads):
             cols = slice(h * W, (h + 1) * W)
-            qp_ref[h] = (mm_nt(queries[:, cols], ku[:, cols]) * SCORE_SCALE).astype(BF16)
-
-    absorb(mail_out)
-
-    def attend(pieces, mask):
+            store[0][h] = (mm_nt(queries[:, cols], ku[:, cols]) * SCORE_SCALE).astype(BF16)
+
+    absorb(mail_out, mine_store)
+
+    def attend(pieces, mask, store):
+        query, top, total_sum, mixed_sum = store
         keys = jnp.concatenate([piece.reshape(line, latent) for piece in pieces], axis=0)
         count = keys.shape[0]
         for b in range(0, heads, GROUP):
             place = slice(b * rows, b * rows + block)
-            queries = qp_ref[b : b + GROUP].reshape(block, latent)
+            queries = query[b : b + GROUP].reshape(block, latent)
             scores = mm_nt(queries, keys)
             if mask is not None:
                 query_pos = here * rows + iota((block, count), 0) % rows
                 scores = jnp.where(mask((1, count)) <= query_pos, scores, -2e30)
-            old = row_max[place, :]
+            old = top[place, :]
             new = jnp.maximum(old, jnp.max(scores, axis=-1, keepdims=True))
-            row_max[place, :] = new
+            top[place, :] = new
             shrink = jnp.exp2(old - new)
             probs = [jnp.exp2(scores[:, c : c + W] - new) for c in range(0, count, W)]
-            added = row_sum[place, :] * shrink
+            added = total_sum[place, :] * shrink
             for p in probs:
                 added = added + p
-            row_sum[place, :] = added
+            total_sum[place, :] = added
             mixed = mm(jnp.concatenate([p.astype(BF16) for p in probs], axis=1), keys)
-            accum[place, :] = accum[place, :] * jnp.concatenate([shrink] * (latent // W), axis=1) + mixed
+            mixed_sum[place, :] = mixed_sum[place, :] * jnp.concatenate([shrink] * (latent // W), axis=1) + mixed
 
     def own_lines(step):
-        u = turn(axes(y)[0], step)
+        u = turn(z, step)
         line_x = turn(x, step)
         return lat_a[0, y, line_x], lat_a[1, y, line_x], lat_b[0, y, u], lat_b[1, y, u]
 
     def own(step):
-        u = turn(axes(y)[0], step)
+        u = turn(z, step)
         line_x = turn(x, step)
 
         def positions(shape):
@@ -548,13 +576,13 @@
             slot, inner, piece = (column // PART) % RING, column % PART, column // line
             part_b = piece // 2
             chip_a = line_x * RING + slot
-            chip_b = jnp.where(y < RING // 2, u * RING + slot, slot * RING + u)
+            chip_b = slot * RING + u
             chip = jnp.where(part_b == 1, chip_b, chip_a)
             return (y * RING * RING + chip) * rows + (piece % 2) * (2 * PART) + part_b * PART + inner
 
         take_a(y, step).wait_recv()
         take_b(y, step).wait_recv()
-        attend(own_lines(step), positions)
+        attend(own_lines(step), positions, mine_store)
 
     def fetch_a(at, step):
         a_from_y(at, step).wait_recv()
@@ -574,80 +602,94 @@
     def loop(begin, end, visit):
         lax.fori_loop(begin, end, lambda i, nothing: (visit(i), nothing)[1], 0)
 
-    lower(spread_b)
-    own(0)
-    for step in others:
+    below = jnp.where(y == RING - 1, 2, jnp.where(y == 0, 0, 1))
+
+    def plane(i):
+        return jnp.where(y == RING - 1, RING - 2 - i // 2, 0)
+
+    def fetch(at, pair):
+        both(pair, lambda step: fetch_a(at, step))
+        both(pair, lambda step: fetch_b(at, step))
+
+    def pass_a(step):
         a_from_x(step).wait_recv()
         spread_a(step)
-    for step in others:
         fetch_b(y, step)
 
+    own(0)
+    lower(spread_b)
+    pass_a(1)
+    pass_a(3)
+
+    @pl.when(y < RING // 2)
+    def _():
+        clear(far_store)
+        mail().wait_recv()
+        absorb(mail_in, far_store)
+
     def own_round(i):
+        pl.when(i == 1)(lambda: pass_a(2))
+        pl.when(jnp.logical_and(i == 2, y > 0))(lambda: fetch(plane(0), 0))
         own(jnp.where(i == 0, 1, jnp.where(i == 1, 3, 2)))
 
+        @pl.when(jnp.logical_and(y < RING // 2, i != 1))
+        def _():
+            first, second = jnp.where(i == 0, 0, 3), jnp.where(i == 0, 1, 2)
+            attend(own_lines(first) + own_lines(second), None, far_store)
+
     loop(0, RING - 1, own_round)
 
-    last_plane = jnp.where(y == RING - 1, 1, 0)
-    pl.when(y > 0)(lambda: both(0, lambda step: fetch_a(y - 1, step)))
-
-    def earlier(i):
-        at, pair = y - 1 - i // 2, i % 2
-        steps = (jnp.where(pair == 0, 0, 3), jnp.where(pair == 0, 1, 2))
-        both(pair, lambda step: fetch_b(at, step))
-        both(pair, lambda step: take_a(at, step).wait_recv())
-        attend([lat_a[c, at, turn(x, step)] for step in steps for c in range(2)], None)
-        following = y - 1 - (i + 1) // 2
-
-        @pl.when(following >= last_plane)
-        def _():
-            both((i + 1) % 2, lambda step: fetch_a(following, step))
-
-        both(pair, lambda step: take_b(at, step).wait_recv())
-        u = axes(at)[0]
-        attend([lat_b[c, at, turn(u, step)] for step in steps for c in range(2)], None)
-
-    loop(0, 2 * (y - last_plane), earlier)
-
     loads[14].wait()
 
-    def result(h):
+    def result(h, store):
         place = slice(h * rows, (h + 1) * rows)
-        row_total = jnp.sum(row_sum[place, :], axis=-1, keepdims=True)
-        high, low = halves(accum[place, :] / row_total)
+        row_total = jnp.sum(store[2][place, :], axis=-1, keepdims=True)
+        high, low = halves(store[3][place, :] / row_total)
         up = vu_ref[:, h * W : (h + 1) * W]
-        return mm(high, up) + mm(low, up), row_max[place, :] + jnp.log2(row_total)
-
-    @pl.when(y < RING - 1)
+        return mm(high, up) + mm(low, up), store[1][place, :] + jnp.log2(row_total)
+
+    @pl.when(y < RING // 2)
     def _():
-        for h in range(heads):
-            out_ref[:, h * W : (h + 1) * W] = result(h)[0].astype(BF16)
-
-    @pl.when(y == 0)
-    def _():
-        mail().wait_recv()
-        absorb(mail_in)
-        clear()
-        loop(0, RING, lambda step: attend(own_lines(step), None))
         lane = iota((rows, W), 1)
         level = jnp.zeros((rows, W), F32)
         for h in range(heads):
-            mixed, log_sum = result(h)
+            mixed, log_sum = result(h, far_store)
             mail_out[:, h * W : (h + 1) * W] = mixed.astype(BF16)
             level = jnp.where(lane == h, log_sum, level)
         note_out[...] = level
         note().start()
         mail().start()
+
+    def earlier(i):
+        at, pair = plane(i), i % 2
+        steps = (jnp.where(pair == 0, 0, 3), jnp.where(pair == 0, 1, 2))
+        pl.when(i + 1 < 2 * below)(lambda: fetch(plane(i + 1), (i + 1) % 2))
+        both(pair, lambda step: take_a(at, step).wait_recv())
+        both(pair, lambda step: take_b(at, step).wait_recv())
+        u = axes(at)[0]
+        attend(
+            [lat_a[c, at, turn(x, step)] for step in steps for c in range(2)]
+            + [lat_b[c, at, turn(u, step)] for step in steps for c in range(2)],
+            None, mine_store,
+        )
+
+    loop(0, 2 * below, earlier)
+
+    @pl.when(y < RING // 2)
+    def _():
+        for h in range(heads):
+            out_ref[:, h * W : (h + 1) * W] = result(h, mine_store)[0].astype(BF16)
         note().wait_send()
         mail().wait_send()
 
-    @pl.when(y == RING - 1)
+    @pl.when(y >= RING // 2)
     def _():
         mail().wait_send()
         note().wait_recv()
         mail().wait_recv()
         for h in range(heads):
             cols = slice(h * W, (h + 1) * W)
-            mixed, log_sum = result(h)
+            mixed, log_sum = result(h, mine_store)
             gap = log_sum - note_in[:, h : h + 1]
             far = mail_in[:, cols].astype(F32)
             out_ref[:, cols] = (
@@ -673,7 +715,8 @@
             give_a(at, step).wait_send()
             give_b(at, step).wait_send()
 
-    loop(last_plane, y + 1, drain)
+    loop(0, below, lambda i: drain(plane(2 * i)))
+    drain(y)
 
 
     for step in range(1, heads):
@@ -706,6 +749,8 @@
         in_specs=[anywhere] * len(operands),
         out_specs=(vm, vm),
         scratch_shapes=[pltpu.VMEM(a.shape, a.dtype) for a in operands] + [
+            pltpu.VMEM((rows, heads * W), F32),
+            pltpu.VMEM((heads, rows, 2 * W), F32),
             pltpu.VMEM((heads,) + message, BF16),
             pltpu.VMEM((rows, heads * W), F32),
             pltpu.VMEM((rows, heads * W), BF16),
@@ -719,6 +764,10 @@
             pltpu.VMEM((heads, rows, latent), BF16),
             pltpu.VMEM((2, RING, RING, RING, PART, latent), BF16),
             pltpu.VMEM((2, RING, RING, RING, PART, latent), BF16),
+            pltpu.VMEM((heads * rows, W), F32),
+            pltpu.VMEM((heads * rows, W), F32),
+            pltpu.VMEM((heads * rows, latent), F32),
+            pltpu.VMEM((heads, rows, latent), BF16),
             pltpu.VMEM((heads * rows, W), F32),
             pltpu.VMEM((heads * rows, W), F32),
             pltpu.VMEM((heads * rows, latent), F32),

time: 83.7 us -> 77 us (0.920)
  Pallas kernels: 82.6 us -> 76.2 us
    pallas_call x1, Pallas kernels: 80.6 us -> 74.2 us  [layer(): pl.pallas_call(layer_kernel, out_shape=(jax.ShapeDtypeStruct((rows, width...]
where the time goes in v5:
time: 77 us; the launch traced here: 76.9 us
  Pallas kernels  76.2 us (99%)
    pallas_call x1, Pallas kernels, layer(): pl.pallas_call(layer_kernel, out_shape=(jax.ShapeDtypeStruct((rows, width...  74.2 us
    pallas_call x1, Pallas kernels, finish(): pl.pallas_call(finish_kernel, out_shape=tuple((jax.ShapeDtypeStruct(a.sha...  2.06 us

profile of v5, /device:TPU:24, one launch (start us, length us, event | category | flops | bytes accessed | tf_op | source)
XLA Modules:
  0.0 76.9 jit_solution(3548786312216284079)
XLA Ops:
  0.6 74.2 %layer.1 = (bf16[128,2304]{1,0:T(8,128)(2,1)}, bf16[128,1024]{1,0:T(8,128)(2,1)}) custom-call(bf16[128,1024]{1,0:T(8,128)(2,1)} %q_hbm.1, bf16[128,1024]{1,0:T(8,128)(2,1)} %k_hbm.1, bf16[128,1024]{1,0:T(8,128)(2,1)} %v_hbm.1, f32[128,1024]{1,0:T(8,128)} %ld_hbm.1, f32[8,128]{1,0:T(8,128)} %bitcast.5, bf16[128,1024]{1,0:T(8,128)(2,1)} %gate_hbm.1, ...), custom_call_target="tpu_custom_call" | custom-call | tf_op jit(solution)/shard_map/layer/pallas_call | solution.py:743
  74.8 2.1 %finish.1 = (bf16[128,2304]{1,0:T(8,128)(2,1)}, bf16[128,1024]{1,0:T(8,128)(2,1)}) custom-call(bf16[128,2304]{1,0:T(8,128)(2,1)} %get-tuple-element.4.hidden_in, bf16[128,1024]{1,0:T(8,128)(2,1)} %get-tuple-element.5.attended_in), custom_call_target="tpu_custom_call" | custom-call | tf_op jit(solution)/shard_map/finish/pallas_call | solution.py:798

commit v6 on v5

--- a/solution.py
+++ b/solution.py
@@ -51,13 +51,14 @@
     return lax.broadcasted_iota(jnp.int32, shape, axis)
 
 
-PIECES = 3
+PIECES = 2
 MESH = pl.DeviceIdType.MESH
 SCORE_SCALE = W ** (-0.5) * 1.4426950408889634
 RING = 4
 PART = 32
 GROUP = 8
 DELTA_GROUP = 8
+SEND_GROUP = 4
 
 
 def pack_diag(closing):
@@ -89,6 +90,12 @@
 def triangle(rows):
     ti, si = iota((rows, rows), 0), iota((rows, rows), 1)
     return ti, si, si < ti
+
+
+def second_rows(x, size):
+    return jnp.concatenate(
+        [x[i + size : i + 2 * size] for i in range(0, x.shape[0], 2 * size)], axis=0
+    )
 
 
 def invert(lowers):
@@ -100,8 +107,34 @@
     size = 2
     while size < rows:
         level = jnp.logical_and((ti // (2 * size)) == (si // (2 * size)), (ti // size) > (si // size))
-        inner = [mm4(jnp.where(level, low, 0.0), x) for low, x in zip(lowers, found)]
-        found = [x - mm4(x, y) for x, y in zip(found, inner)]
+        inside = [jnp.where(level, low, 0.0) for low in lowers]
+        if size < 8:
+            inner = [mm4(low, x) for low, x in zip(inside, found)]
+            found = [x - mm4(x, y) for x, y in zip(found, inner)]
+        else:
+            zero = jnp.zeros((size, rows), F32)
+            inner = [mm4(second_rows(low, size), x) for low, x in zip(inside, found)]
+            inner = [
+                jnp.concatenate(
+                    [part for i in range(0, rows // 2, size) for part in (zero, y[i : i + size])], axis=0
+                )
+                for y in inner
+            ]
+            change = [mm4(second_rows(x, size), y) for x, y in zip(found, inner)]
+            found = [
+                jnp.concatenate(
+                    [
+                        part
+                        for i in range(0, rows // 2, size)
+                        for part in (
+                            x[2 * i : 2 * i + size],
+                            x[2 * i + size : 2 * i + 2 * size] - y[i : i + size],
+                        )
+                    ],
+                    axis=0,
+                )
+                for x, y in zip(found, change)
+            ]
         size *= 2
     return found
 
@@ -112,14 +145,15 @@
     ti, si, strict = triangle(rows)
     ones = jnp.where(si <= ti, 1.0, 0.0).astype(BF16)
     rates = (1.0 / (1.0 + jnp.exp(-beta_ref[...]))).T
+    ld = ld_ref[...]
+    high, rest = halves(ld)
+    low = (ld - high.astype(F32) - rest.astype(F32)).astype(BF16)
+    twice = jnp.concatenate([ones, ones], axis=1)
+    cum_ref[...] = mm(twice, jnp.concatenate([high, rest], axis=0)) + mm(ones, low)
 
     def prepare(h):
         cols = slice(h * W, (h + 1) * W)
-        ld = ld_ref[:, cols]
-        high, rest = halves(ld)
-        low = (ld - high.astype(F32) - rest.astype(F32)).astype(BF16)
-        cum = mm(ones, high) + (mm(ones, rest) + mm(ones, low))
-        cum_ref[:, cols] = cum
+        cum = cum_ref[:, cols]
         mid = cum[rows // 2 - 1 : rows // 2, :]
         end = cum[rows - 1 : rows, :]
         key = unit(k_ref[:, cols].astype(F32))
@@ -143,7 +177,8 @@
             msg_ref[h, :W, :W] = state[:, W:].astype(BF16)
             msg_ref[h, :W, W:] = state[:, :W].astype(BF16)
             msg_ref[h, W:, :] = pack_diag(closing)
-        sent(start, start + DELTA_GROUP)
+            if (h + 1) % SEND_GROUP == 0:
+                sent(h + 1 - SEND_GROUP, h + 1)
 
 
 def delta_outputs(q_ref, k_ref, cum_ref, solved_ref, base_ref, carry_ref):
@@ -454,7 +489,7 @@
     def take_b(at, step):
         return remote(lat_b.at[1 - core, at, turn(axes(at)[0], step)], sibling, swap_b.at[at, step], got_b.at[at, step])
 
-    others = (1, 3, 2)
+    others = (2, 1, 3)
 
     partner = device(RING - 1 - y, x, z)
 
@@ -644,9 +679,10 @@
     def result(h, store):
         place = slice(h * rows, (h + 1) * rows)
         row_total = jnp.sum(store[2][place, :], axis=-1, keepdims=True)
-        high, low = halves(store[3][place, :] / row_total)
+        high, low = halves(store[3][place, :] * (1.0 / row_total))
         up = vu_ref[:, h * W : (h + 1) * W]
-        return mm(high, up) + mm(low, up), store[1][place, :] + jnp.log2(row_total)
+        both_parts = mm(jnp.concatenate([high, low], axis=0), up)
+        return both_parts[:rows] + both_parts[rows:], store[1][place, :] + jnp.log2(row_total)
 
     @pl.when(y < RING // 2)
     def _():

time: 77 us -> 76.5 us (level)
  no operation moved by 1% of the time
where the time goes in v6:
time: 76.5 us; the launch traced here: 76.3 us
  Pallas kernels  75.7 us (99%)
    pallas_call x1, Pallas kernels, layer(): pl.pallas_call(layer_kernel, out_shape=(jax.ShapeDtypeStruct((rows, width...  73.6 us
    pallas_call x1, Pallas kernels, finish(): pl.pallas_call(finish_kernel, out_shape=tuple((jax.ShapeDtypeStruct(a.sha...  2.06 us

profile of v6, /device:TPU:24, one launch (start us, length us, event | category | flops | bytes accessed | tf_op | source)
XLA Modules:
  0.0 76.3 jit_solution(15405967798177085735)
XLA Ops:
  0.6 73.6 %layer.1 = (bf16[128,2304]{1,0:T(8,128)(2,1)}, bf16[128,1024]{1,0:T(8,128)(2,1)}) custom-call(bf16[128,1024]{1,0:T(8,128)(2,1)} %q_hbm.1, bf16[128,1024]{1,0:T(8,128)(2,1)} %k_hbm.1, bf16[128,1024]{1,0:T(8,128)(2,1)} %v_hbm.1, f32[128,1024]{1,0:T(8,128)} %ld_hbm.1, f32[8,128]{1,0:T(8,128)} %bitcast.5, bf16[128,1024]{1,0:T(8,128)(2,1)} %gate_hbm.1, ...), custom_call_target="tpu_custom_call" | custom-call | tf_op jit(solution)/shard_map/layer/pallas_call | solution.py:779
  74.2 2.1 %finish.1 = (bf16[128,2304]{1,0:T(8,128)(2,1)}, bf16[128,1024]{1,0:T(8,128)(2,1)}) custom-call(bf16[128,2304]{1,0:T(8,128)(2,1)} %get-tuple-element.4.hidden_in, bf16[128,1024]{1,0:T(8,128)(2,1)} %get-tuple-element.5.attended_in), custom_call_target="tpu_custom_call" | custom-call | tf_op jit(solution)/shard_map/finish/pallas_call | solution.py:834

commit v7 on v6

--- a/solution.py
+++ b/solution.py
@@ -293,25 +293,38 @@
     total[:W, W:] = whole[:, W:].astype(BF16)
     total[W:, :] = pack_diag(diag)
 
-    def send_total(step):
+    def total_copy(peer, slot, device, first):
+        place = (slice(0, W), slice(W, 2 * W)) if first else (slice(None), slice(None))
+        return pltpu.make_async_remote_copy(
+            src_ref=total.at[place], dst_ref=totals.at[(slot,) + place],
+            send_sem=send_b.at[peer], recv_sem=recv_b.at[slot],
+            device_id=device, device_id_type=MESH,
+        )
+
+    def each_total(step, action):
         peer, device = cousin(step)
-        return peer, pltpu.make_async_remote_copy(
-            src_ref=total, dst_ref=totals.at[mine],
-            send_sem=send_b.at[peer], recv_sem=recv_b.at[mine],
-            device_id=device, device_id_type=MESH,
-        )
+
+        @pl.when(jnp.logical_and(peer > mine, mine == 0))
+        def _():
+            action(total_copy(peer, mine, device, True))
+
+        @pl.when(jnp.logical_and(peer > mine, mine > 0))
+        def _():
+            action(total_copy(peer, mine, device, False))
 
     def take_total(step):
         peer, device = cousin(step)
-        return peer, pltpu.make_async_remote_copy(
-            src_ref=total, dst_ref=totals.at[peer],
-            send_sem=send_b.at[peer], recv_sem=recv_b.at[peer],
-            device_id=device, device_id_type=MESH,
-        )
+
+        @pl.when(jnp.logical_and(peer < mine, peer == 0))
+        def _():
+            total_copy(peer, peer, device, True).wait_recv()
+
+        @pl.when(jnp.logical_and(peer < mine, peer > 0))
+        def _():
+            total_copy(peer, peer, device, False).wait_recv()
 
     for step in range(1, groups):
-        peer, copy = send_total(step)
-        pl.when(peer > mine)(copy.start)
+        each_total(step, lambda copy: copy.start())
 
     before = [None] * heads
     before[1] = maps[0]
@@ -323,8 +336,7 @@
     before[7] = after(maps[6], before[6])
 
     for step in range(1, groups):
-        peer, copy = take_total(step)
-        pl.when(peer < mine)(copy.wait_recv)
+        take_total(step)
 
     eye_zero = jnp.concatenate([jnp.where(eye, 1.0, 0.0), jnp.zeros((W, W), F32)], axis=1)
     chain = [jnp.where(j < mine, unpack_map(totals[j])[0], eye_zero) for j in range(groups - 1)]
@@ -759,8 +771,7 @@
         map_to(member(step)[0]).wait_send()
         send_state(step).wait_send()
     for step in range(1, groups):
-        peer, copy = send_total(step)
-        pl.when(peer > mine)(copy.wait_send)
+        each_total(step, lambda copy: copy.wait_send())
     for p in range(PIECES):
         swap(p).wait_send()
 

time: 76.5 us -> 76.1 us (level)
  no operation moved by 1% of the time
where the time goes in v7:
time: 76.1 us; the launch traced here: 75.6 us
  Pallas kernels  75 us (99%)
    pallas_call x1, Pallas kernels, layer(): pl.pallas_call(layer_kernel, out_shape=(jax.ShapeDtypeStruct((rows, width...  72.9 us
    pallas_call x1, Pallas kernels, finish(): pl.pallas_call(finish_kernel, out_shape=tuple((jax.ShapeDtypeStruct(a.sha...  2.06 us

profile of v7, /device:TPU:24, one launch (start us, length us, event | category | flops | bytes accessed | tf_op | source)
XLA Modules:
  0.0 75.6 jit_solution(1682039662875508900)
XLA Ops:
  0.6 72.9 %layer.1 = (bf16[128,2304]{1,0:T(8,128)(2,1)}, bf16[128,1024]{1,0:T(8,128)(2,1)}) custom-call(bf16[128,1024]{1,0:T(8,128)(2,1)} %q_hbm.1, bf16[128,1024]{1,0:T(8,128)(2,1)} %k_hbm.1, bf16[128,1024]{1,0:T(8,128)(2,1)} %v_hbm.1, f32[128,1024]{1,0:T(8,128)} %ld_hbm.1, f32[8,128]{1,0:T(8,128)} %bitcast.5, bf16[128,1024]{1,0:T(8,128)(2,1)} %gate_hbm.1, ...), custom_call_target="tpu_custom_call" | custom-call | tf_op jit(solution)/shard_map/layer/pallas_call | solution.py:790
  73.6 2.1 %finish.1 = (bf16[128,2304]{1,0:T(8,128)(2,1)}, bf16[128,1024]{1,0:T(8,128)(2,1)}) custom-call(bf16[128,2304]{1,0:T(8,128)(2,1)} %get-tuple-element.4.hidden_in, bf16[128,1024]{1,0:T(8,128)(2,1)} %get-tuple-element.5.attended_in), custom_call_target="tpu_custom_call" | custom-call | tf_op jit(solution)/shard_map/finish/pallas_call | solution.py:845
